TPU v7x, 32 devices: a whole 2x2x4 slice. The times are simulated.
32 devices in a mesh: shard: 32 (over z, y, x, core).
Axes of the slice: x: 2, y: 2, z: 4, core: 2. Of those that a mesh axis runs over, the one named last changes fastest.
Arguments:
- features: bfloat16 [163840, 400], P('shard'), may hold values from -6 to 6
- counts: int32 [32], P('shard'), may hold values from 1706 to 5120, as said below
- labelled: int32 [163840], P('shard'), may hold values from 0 to 1, as said below
- labels: int32 [163840], P('shard'), may hold values from 0 to 46
- w_branch: float32 [400, 512], P(None, 'shard'), may hold values from -0.625 to 0.625
- w_mid: float32 [2048, 512], P(None, 'shard'), may hold values from -0.125 to 0.125
- w_head: float32 [512, 47], replicated, may hold values from -0.25 to 0.25
- small_params: float32 [9775], replicated, as said below
- mom_branch: float32 [400, 512], P(None, 'shard'), may hold values from -16 to 16
- mom_mid: float32 [2048, 512], P(None, 'shard'), may hold values from -28 to 28
- mom_head: float32 [512, 47], replicated, may hold values from -3072 to 3072
- mom_small: float32 [9775], replicated, may hold values from -20 to 20
- avg_branch: float32 [400, 512], P(None, 'shard'), may hold values from -0.625 to 0.625
- avg_mid: float32 [2048, 512], P(None, 'shard'), may hold values from -0.125 to 0.125
- avg_head: float32 [512, 47], replicated, may hold values from -0.25 to 0.25
- avg_small: float32 [9775], replicated, may hold values from -3 to 3
Outputs:
- logits: float32 [163840, 47], P('shard')
- features_grad: float32 [163840, 400], P('shard')
- grad_branch: float32 [400, 512], P(None, 'shard')
- grad_mid: float32 [2048, 512], P(None, 'shard')
- grad_head: float32 [512, 47], replicated
- grad_small: float32 [9775], replicated
- new_mom_branch: float32 [400, 512], P(None, 'shard')
- new_mom_mid: float32 [2048, 512], P(None, 'shard')
- new_mom_head: float32 [512, 47], replicated
- new_mom_small: float32 [9775], replicated
- new_avg_branch: float32 [400, 512], P(None, 'shard')
- new_avg_mid: float32 [2048, 512], P(None, 'shard')
- new_avg_head: float32 [512, 47], replicated
- new_avg_small: float32 [9775], replicated
- new_branch: float32 [400, 512], P(None, 'shard')
- new_mid: float32 [2048, 512], P(None, 'shard')
- new_head: float32 [512, 47], replicated
- new_small: float32 [9775], replicated
Inputs may be any that keep to these rules, and one draw needn't show every extreme that they name: `counts`: filled slots of each device's bucket; some device's bucket is full in every draw. `labelled`: the first slot of every device's bucket is a training node. `small_params`: gains near one, shifts and class bias of both signs, slopes between 0.05 and 0.45.
All inputs are finite; a program needn't handle non-finite values.
Results may differ from a plain program's by a relative error of at most 0.0076.
Values may be sent and summed in bfloat16 or wider, within the bound.
A program may use at most 320 MiB of HBM per device.

v0:
```python
import math

import jax
import jax.numpy as jnp
from jax import lax
from jax.sharding import PartitionSpec as P

K = 4
F = 100
H = 512
C = 47


EPS = 1e-05
MOMENTUM = 0.9
DECAY = 0.9


def prelu_apply(values_in, slopes):
    return slopes * values_in + (1.0 - slopes) * jax.nn.softplus(values_in)


def prelu_slope_term(values_in):
    return values_in - jax.nn.softplus(values_in)


def prelu_input_factor(values_in, slopes):
    return slopes + (1.0 - slopes) * jax.nn.sigmoid(values_in)


def split_small(packed):
    width = K * H
    return (
        packed[:width],
        packed[width : 2 * width],
        packed[2 * width : 3 * width],
        packed[3 * width : 4 * width],
        packed[4 * width : 4 * width + H],
        packed[4 * width + H : 4 * width + 2 * H],
        packed[4 * width + 2 * H : 4 * width + 3 * H],
        packed[4 * width + 3 * H :],
    )


def nesterov(weight, gradient, momentum_old, average_old, step_rate):
    momentum_new = MOMENTUM * momentum_old + gradient
    weight_new = weight - step_rate * (gradient + MOMENTUM * momentum_new)
    average_new = DECAY * average_old + (1.0 - DECAY) * weight_new
    return (momentum_new, average_new, weight_new)


def moments(columns_in, bucket):
    masked = columns_in * bucket[:, None]
    totals, count_fill = lax.psum((jnp.sum(masked, axis=0), jnp.sum(bucket)), "shard")
    mean_col = totals / count_fill
    centered = columns_in - mean_col
    squares = lax.psum(jnp.sum(centered * centered * bucket[:, None], axis=0), "shard")
    variance = squares / count_fill
    return (mean_col, lax.rsqrt(variance + EPS), count_fill)


def local(
    features,
    counts,
    labelled,
    labels,
    w_branch,
    w_mid,
    w_head,
    small_params,
    mom_branch,
    mom_mid,
    mom_head,
    mom_small,
    avg_branch,
    avg_mid,
    avg_head,
    avg_small,
):
    node_rows = features.shape[0]
    nodes_all = node_rows * lax.axis_size("shard")
    gain1, shift1, slope1, slope2, gain2, shift2, slope3, head_bias = split_small(small_params)
    slot_index = lax.broadcasted_iota(jnp.int32, (node_rows,), 0)
    bucket = (slot_index < counts[0]).astype(jnp.float32)
    trained = bucket * labelled.astype(jnp.float32)
    branch_low = w_branch.astype(jnp.bfloat16)
    mid_low = w_mid.astype(jnp.bfloat16)
    head_low = w_head.astype(jnp.bfloat16)
    branch_full = lax.all_gather(branch_low, "shard", axis=1, tiled=True)
    feats_three = features.reshape(node_rows, K, F)
    branch_three = branch_full.reshape(K, F, H)
    branch_pre = jnp.einsum(
        "nkf,kfh->nkh", feats_three, branch_three, preferred_element_type=jnp.float32
    ).reshape(node_rows, K * H)
    mean1, inv1, count_fill = moments(branch_pre, bucket)
    branch_hat = (branch_pre - mean1) * inv1
    branch_norm = gain1 * branch_hat + shift1
    branch_act = prelu_apply(branch_norm, slope1)
    concat_low = prelu_apply(branch_act, slope2).astype(jnp.bfloat16)
    mid_full = lax.all_gather(mid_low, "shard", axis=1, tiled=True)
    mid_pre = jnp.dot(concat_low, mid_full, preferred_element_type=jnp.float32)
    mean2, inv2, unused_fill = moments(mid_pre, bucket)
    mid_hat = (mid_pre - mean2) * inv2
    mid_norm = gain2 * mid_hat + shift2
    hidden_low = prelu_apply(mid_norm, slope3).astype(jnp.bfloat16)
    scores = jnp.dot(hidden_low, head_low, preferred_element_type=jnp.float32) + head_bias
    log_total = jax.nn.logsumexp(scores, axis=1)
    prob_rows = jnp.exp(scores - log_total[:, None])
    one_hot = (labels[:, None] == lax.broadcasted_iota(jnp.int32, (1, C), 1)).astype(jnp.float32)
    logit_low = ((prob_rows - one_hot) * trained[:, None]).astype(jnp.bfloat16)
    head_part = jnp.dot(hidden_low.T, logit_low, preferred_element_type=jnp.float32)
    bias_part = jnp.sum(logit_low.astype(jnp.float32), axis=0)
    hidden_grad = jnp.dot(logit_low, head_low.T, preferred_element_type=jnp.float32)
    slope_out_part = jnp.sum(hidden_grad * prelu_slope_term(mid_norm), axis=0)
    mid_norm_grad = hidden_grad * prelu_input_factor(mid_norm, slope3)
    grad_head, grad_bias, grad_slope3, grad_gain2, grad_shift2 = lax.psum(
        (
            head_part,
            bias_part,
            slope_out_part,
            jnp.sum(mid_norm_grad * mid_hat * bucket[:, None], axis=0),
            jnp.sum(mid_norm_grad * bucket[:, None], axis=0),
        ),
        "shard",
    )
    mid_grad_low = (
        gain2
        * inv2
        * bucket[:, None]
        * (mid_norm_grad - (grad_shift2 + mid_hat * grad_gain2) / count_fill)
    ).astype(jnp.bfloat16)
    mid_part = jnp.dot(concat_low.T, mid_grad_low, preferred_element_type=jnp.float32)
    concat_grad = jnp.dot(mid_grad_low, mid_full.T, preferred_element_type=jnp.float32)
    slope_two_part = jnp.sum(concat_grad * prelu_slope_term(branch_act), axis=0)
    act_grad = concat_grad * prelu_input_factor(branch_act, slope2)
    slope_one_part = jnp.sum(act_grad * prelu_slope_term(branch_norm), axis=0)
    norm_grad = act_grad * prelu_input_factor(branch_norm, slope1)
    grad_slope1, grad_slope2, grad_gain1, grad_shift1 = lax.psum(
        (
            slope_one_part,
            slope_two_part,
            jnp.sum(norm_grad * branch_hat * bucket[:, None], axis=0),
            jnp.sum(norm_grad * bucket[:, None], axis=0),
        ),
        "shard",
    )
    branch_grad_low = (
        gain1
        * inv1
        * bucket[:, None]
        * (norm_grad - (grad_shift1 + branch_hat * grad_gain1) / count_fill)
    ).astype(jnp.bfloat16)
    branch_grad_three = branch_grad_low.reshape(node_rows, K, H)
    features_grad = jnp.einsum(
        "nkh,kfh->nkf", branch_grad_three, branch_three, preferred_element_type=jnp.float32
    ).reshape(node_rows, K * F)
    branch_part = jnp.einsum(
        "nkf,nkh->kfh", feats_three, branch_grad_three, preferred_element_type=jnp.float32
    ).reshape(K * F, H)
    grad_branch, grad_mid = (
        lax.psum_scatter(branch_part, "shard", scatter_dimension=1, tiled=True),
        lax.psum_scatter(mid_part, "shard", scatter_dimension=1, tiled=True),
    )
    grad_small = jnp.concatenate(
        [
            grad_gain1,
            grad_shift1,
            grad_slope1,
            grad_slope2,
            grad_gain2,
            grad_shift2,
            grad_slope3,
            grad_bias,
        ]
    )
    root = math.sqrt(nodes_all)
    mom_b, avg_b, new_b = nesterov(w_branch, grad_branch, mom_branch, avg_branch, 0.8 / root)
    mom_m, avg_m, new_m = nesterov(w_mid, grad_mid, mom_mid, avg_mid, 0.08 / root)
    mom_h, avg_h, new_h = nesterov(w_head, grad_head, mom_head, avg_head, 0.3 / root)
    mom_s, avg_s, new_s = nesterov(small_params, grad_small, mom_small, avg_small, 1.0 / root)
    logits = scores * bucket[:, None]
    return (
        logits,
        features_grad,
        grad_branch,
        grad_mid,
        grad_head,
        grad_small,
        mom_b,
        mom_m,
        mom_h,
        mom_s,
        avg_b,
        avg_m,
        avg_h,
        avg_s,
        new_b,
        new_m,
        new_h,
        new_s,
    )


def solution(mesh):
    in_specs = (
        P("shard", None),
        P("shard"),
        P("shard"),
        P("shard"),
        P(None, "shard"),
        P(None, "shard"),
        P(),
        P(),
        P(None, "shard"),
        P(None, "shard"),
        P(),
        P(),
        P(None, "shard"),
        P(None, "shard"),
        P(),
        P(),
    )
    out_specs = (
        P("shard", None),
        P("shard", None),
        P(None, "shard"),
        P(None, "shard"),
        P(),
        P(),
        P(None, "shard"),
        P(None, "shard"),
        P(),
        P(),
        P(None, "shard"),
        P(None, "shard"),
        P(),
        P(),
        P(None, "shard"),
        P(None, "shard"),
        P(),
        P(),
    )
    return jax.shard_map(local, mesh=mesh, in_specs=in_specs, out_specs=out_specs, check_vma=False)
```

profile of v0, /device:TPU:0, one launch (start us, length us, event | category | flops | bytes accessed | tf_op | source)
XLA Modules:
  0.0 917.7 jit_solution(16101625293680502912)
XLA Ops:
  7.2 1.5 convert_element_type.43
  8.8 0.0 all-reduce.5.cloned.1.call-start
  9.5 0.6 fusion.9
  10.1 0.7 slice.31
  10.8 0.8 convert_element_type.40
  11.6 44.7 %all_gather.6 = bf16[400,512]{0,1:T(8,128)(2,1)S(1)} all-gather(bf16[400,16]{0,1:T(8,128)(2,1)S(1)} %convert_element_type.40), channel_id=1, replica_groups=mesh['shard'=32] {'shard'}, dimensions={1}, use_global_device_ids=true | all-gather | bytes 422400 | tf_op jit(solution)/shard_map/all_gather | solution.py:89
  56.3 0.2 copy.62
  56.5 0.1 reshape.109
  56.6 4.1 reshape.110
  60.7 18.7 %fusion.4 = (f32[4,512]{1,0:T(4,128)S(1)}, f32[4,512,5120]{2,1,0:T(8,128)}) fusion(f32[5120]{0:T(1024)S(1)} %fusion.8, bf16[4,100,512]{2,1,0:T(8,128)(2,1)S(1)} %reshape.109, bf16[5120,4,100]{0,2,1:T(8,128)(2,1)} %reshape.110), kind=kOutput, calls=%fused_computation.9 | convolution fusion | flops 2118121472 | bytes 46477312 | tf_op jit(solution)/shard_map/nkf,kfh->nkh/dot_general | solution.py:92
  79.4 37.1 %all-reduce.2 = (f32[2048]{0:T(1024)S(1)}, f32[]{:T(128)}) all-reduce(f32[2048]{0:T(1024)S(1)} %bitcast.70, f32[]{:T(128)} %fusion.9), channel_id=1, replica_groups=mesh['shard'=32] {'shard'}, use_global_device_ids=true, to_apply=%region_1.0 | all-reduce | flops 2049 | bytes 16392 | tf_op jit(solution)/shard_map/psum | solution.py:54
  116.5 0.6 broadcast_divide_fusion
  117.2 16.8 %fusion.3 = f32[4,512]{1,0:T(4,128)S(1)} fusion(f32[4,512,5120]{2,1,0:T(8,128)} %get-tuple-element.129, f32[4,512]{1,0:T(4,128)S(1)} %sub.91, f32[5120]{0:T(1024)S(1)} %fusion.8), kind=kLoop, calls=%fused_computation.8 | loop fusion | flops 41940992 | bytes 41979904 | tf_op jit(solution)/shard_map/reduce_sum | solution.py:57
  134.0 41.9 %psum.103 = f32[2048]{0:T(1024)S(1)} all-reduce(f32[2048]{0:T(1024)S(1)} %bitcast.71), channel_id=1, replica_groups=mesh['shard'=32] {'shard'}, use_global_device_ids=true, to_apply=%region_5.0 | all-reduce | flops 2048 | bytes 16384 | tf_op jit(solution)/shard_map/psum | solution.py:57
  175.9 1.3 fusion.11
  177.2 66.5 %add_convert_fusion = (bf16[5120,2048]{0,1:T(8,128)(2,1)}, f32[5120,2048]{0,1:T(8,128)}) fusion(f32[2048]{0:T(1024)S(1)} %get-tuple-element.121, f32[2048]{0:T(1024)S(1)} %get-tuple-element.127, f32[2048]{0:T(1024)S(1)} %get-tuple-element.122, f32[2048]{0:T(1024)S(1)} %get-tuple-element.125, f32[2048]{0:T(1024)S(1)} %get-tuple-element.124, ...), kind=kLoop, calls=%fused_computation.17 | loop fusion | flops 241172480 | bytes 104923136 | tf_op jit(solution)/shard_map/convert_element_type | solution.py:99
  243.7 20.4 %multiply_reduce_fusion.8 = (f32[512]{0:T(512)S(1)}, f32[5120,512]{1,0:T(8,128)}) fusion(f32[5120]{0:T(1024)S(1)} %fusion.8, bf16[5120,2048]{0,1:T(8,128)(2,1)} %get-tuple-element.108, bf16[2048,512]{0,1:T(8,128)(2,1)} %all-gather.2.cloned.1.call-done), kind=kOutput, calls=%fused_computation.29 | convolution fusion | flops 10742661120 | bytes 33576960 | tf_op jit(solution)/shard_map/dot_general | solution.py:101
  264.0 39.5 %psum.104 = f32[512]{0:T(512)S(1)} all-reduce(f32[512]{0:T(512)S(1)} %get-tuple-element.130), channel_id=1, replica_groups=mesh['shard'=32] {'shard'}, use_global_device_ids=true, to_apply=%region_7.8 | all-reduce | flops 512 | bytes 4096 | tf_op jit(solution)/shard_map/psum | solution.py:54
  303.6 0.6 broadcast_divide_fusion.1
  304.2 5.6 multiply_reduce_fusion.7
  309.8 40.7 %psum.105 = f32[512]{0:T(512)S(1)} all-reduce(f32[512]{0:T(512)S(1)} %multiply_reduce_fusion.7), channel_id=1, replica_groups=mesh['shard'=32] {'shard'}, use_global_device_ids=true, to_apply=%region_9.10 | all-reduce | flops 512 | bytes 4096 | tf_op jit(solution)/shard_map/psum | solution.py:57
  350.4 0.7 fusion.10
  351.1 10.0 %add_convert_fusion.1 = bf16[5120,512]{1,0:T(8,128)(2,1)S(1)} fusion(f32[5120,512]{1,0:T(8,128)} %get-tuple-element.131, f32[512]{0:T(512)S(1)} %get-tuple-element.115, f32[512]{0:T(512)S(1)} %get-tuple-element.118, f32[512]{0:T(512)S(1)} %get-tuple-element.117, f32[512]{0:T(512)S(1)} %broadcast_divide_fusion.1, f32[512]{0:T(512)S(1)} %get-tuple-element.119, ...), kind=kLoop, calls=%fused_computation.26 | loop fusion | flops 36700160 | bytes 15740928 | tf_op jit(solution)/shard_map/convert_element_type | solution.py:105
  361.2 1.6 fusion.12
  362.8 0.2 exponential_reduce_fusion
  363.0 1.9 convert_reduce_fusion
  364.9 1.6 fusion.14
  366.6 16.2 %multiply_reduce_fusion.6 = (f32[512]{0:T(512)S(1)}, f32[512]{0:T(512)S(1)}, f32[512]{0:T(512)}, f32[5120,512]{1,0:T(8,128)}) fusion(f32[5120]{0:T(1024)S(1)} %fusion.8, f32[512]{0:T(512)S(1)} %get-tuple-element.118, f32[512]{0:T(512)S(1)} %get-tuple-element.117, f32[5120,512]{1,0:T(8,128)} %get-tuple-element.131, f32[512]{0:T(512)S(1)} %broadcast_divide_fusion.1, ...), kind=kOutput, calls=%fused_computation.24 | convolution fusion | flops 309352448 | bytes 21587968 | tf_op jit(solution)/shard_map/dot_general | solution.py:113
  382.8 0.0 reduce-scatter.7.cloned.1.call-start
  382.8 39.8 %all-reduce.1 = (f32[512]{0:T(512)S(1)}, f32[512]{0:T(512)S(1)}) all-reduce(f32[512]{0:T(512)S(1)} %get-tuple-element.77, f32[512]{0:T(512)S(1)} %get-tuple-element.76), channel_id=1, replica_groups=mesh['shard'=32] {'shard'}, use_global_device_ids=true, to_apply=%region_15.16 | all-reduce | flops 1024 | bytes 8192 | tf_op jit(solution)/shard_map/psum | solution.py:116
  422.6 11.1 %multiply_convert_fusion.1 = bf16[5120,512]{1,0:T(8,128)(2,1)S(1)} fusion(f32[5120,512]{1,0:T(8,128)} %get-tuple-element.131, f32[]{:T(128)} %get-tuple-element.88, f32[512]{0:T(512)S(1)} %get-tuple-element.85, f32[512]{0:T(512)S(1)} %get-tuple-element.86, f32[512]{0:T(512)S(1)} %get-tuple-element.116, f32[512]{0:T(512)S(1)} %get-tuple-element.117, ...), kind=kLoop, calls=%fused_computation.22 | loop fusion | flops 44564480 | bytes 26253316 | tf_op jit(solution)/shard_map/convert_element_type | solution.py:131
  433.8 109.1 %multiply_reduce_fusion = (f32[2048]{0:T(1024)S(1)}, f32[2048]{0:T(1024)S(1)}, f32[2048]{0:T(1024)S(1)}, f32[2048]{0:T(1024)S(1)}, f32[5120,2048]{0,1:T(8,128)}) fusion(f32[5120,2048]{0,1:T(8,128)} %get-tuple-element.109, f32[2048]{0:T(1024)S(1)} %get-tuple-element.125, f32[2048]{0:T(1024)S(1)} %get-tuple-element.124, f32[2048]{0:T(1024)S(1)} %broadcast_divide_fusion, ...), kind=kOutput, calls=%fused_computation.10 | convolution fusion | flops 11146354688 | bytes 133287936 | tf_op jit(solution)/shard_map/dot_general | solution.py:133
  542.9 41.4 %all-reduce = (f32[2048]{0:T(1024)S(1)}, f32[2048]{0:T(1024)S(1)}, f32[2048]{0:T(1024)S(1)}, f32[2048]{0:T(1024)S(1)}, f32[512]{0:T(512)S(1)}, /*index=5*/f32[47]{0:T(128)S(1)}) all-reduce(f32[2048]{0:T(1024)S(1)} %get-tuple-element.110, f32[2048]{0:T(1024)S(1)} %get-tuple-element.111, ...), channel_id=1, replica_groups=mesh['shard'=32] {'shard'}, use_global_device_ids=true, to_apply=%region_19.20 | all-reduce | flops 8751 | bytes 70008 | tf_op jit(solution)/shard_map/psum | solution.py:138
  584.3 34.9 %multiply_convert_fusion = bf16[5120,2048]{0,1:T(8,128)(2,1)} fusion(f32[5120,2048]{0,1:T(8,128)} %get-tuple-element.112, f32[4,512,5120]{2,1,0:T(8,128)} %get-tuple-element.129, f32[]{:T(128)} %get-tuple-element.88, f32[2048]{0:T(1024)S(1)} %get-tuple-element.79, f32[2048]{0:T(1024)S(1)} %get-tuple-element.80, f32[5120]{0:T(1024)S(1)} %fusion.8, ...), kind=kLoop, calls=%fused_computation.12 | loop fusion | flops 94371840 | bytes 104919040 | tf_op jit(solution)/shard_map/convert_element_type | solution.py:152
  619.2 12.0 %convolution_bitcast_fusion.1 = f32[4,100,512]{2,1,0:T(8,128)S(1)} fusion(bf16[5120,4,512]{0,2,1:T(8,128)(2,1)} %bitcast.64, bf16[5120,4,100]{0,2,1:T(8,128)(2,1)} %reshape.110), kind=kOutput, calls=%fused_computation.33 | convolution fusion | flops 2097152000 | bytes 25886720 | tf_op jit(solution)/shard_map/nkf,nkh->kfh/dot_general | solution.py:157
  631.2 0.1 reshape.114
  631.3 1.4 copy.70
  632.7 0.0 reduce-scatter.5.cloned.1.call-start
  632.8 18.3 %fusion.13 = f32[2048,512]{0,1:T(8,128)} fusion(bf16[5120,2048]{0,1:T(8,128)(2,1)} %get-tuple-element.108, bf16[5120,512]{1,0:T(8,128)(2,1)} %copy-done), kind=kOutput, calls=%fused_computation.80 | convolution fusion | flops 10737418240 | bytes 30408704 | tf_op jit(solution)/shard_map/dot_general | solution.py:132
  651.1 11.3 %convolution_bitcast_fusion = f32[5120,4,100]{0,2,1:T(8,128)} fusion(bf16[5120,4,512]{0,2,1:T(8,128)(2,1)} %bitcast.65, bf16[4,100,512]{2,1,0:T(8,128)(2,1)S(1)} %copy-done.2), kind=kOutput, calls=%fused_computation.31 | convolution fusion | flops 2097152000 | bytes 29573120 | tf_op jit(solution)/shard_map/nkh,kfh->nkf/dot_general | solution.py:154
  662.6 9.4 %reshape.113 = f32[5120,400]{0,1:T(8,128)} reshape(f32[5120,4,100]{0,2,1:T(8,128)} %convolution_bitcast_fusion) | data formatting | bytes 16384000 | tf_op jit(solution)/shard_map/reshape | solution.py:156
  672.1 0.7 multiply_add_fusion.7
  672.8 1.6 multiply_add_fusion.5
  674.4 93.2 %reduce-scatter.7.cloned.1.call-done = f32[16,400]{1,0:T(8,128)} async-done(((f32[512,400]{1,0:T(8,128)}), f32[16,400]{1,0:T(8,128)}) %reduce-scatter.7.cloned.1.call-update) | async-done | bytes 25616
  767.7 1.4 multiply_add_fusion.9
  769.1 138.4 %reduce-scatter.5.cloned.1.call-done = f32[2048,16]{0,1:T(8,128)} async-done(((f32[2048,512]{0,1:T(8,128)}), f32[2048,16]{0,1:T(8,128)}) %reduce-scatter.5.cloned.1.call-update) | async-done | bytes 131088 | tf_op jit(solution)/shard_map/reduce_scatter | solution.py:162
  907.4 1.7 multiply_add_fusion.3
  909.1 1.5 copy.83
  (76 shorter events, 0.3 us)
Async XLA Ops:
  7.2 236.5 %all-gather.2.cloned.1.call-start = ((), (), s32[]{:S(2)}) async-start(), calls=%async_computation.2 | async-start | bytes 2162688 | tf_op jit(solution)/shard_map/all_gather | solution.py:100
  8.8 664.0 %all-reduce.5.cloned.1.call-start = ((), (), s32[]{:S(2)}) async-start(), calls=%async_computation.4 | async-start | bytes 196608 | tf_op jit(solution)/shard_map/psum | solution.py:116
  56.6 22.8 %copy-start.1 = (bf16[4,100,512]{2,1,0:T(8,128)(2,1)}, bf16[4,100,512]{2,1,0:T(8,128)(2,1)S(1)}, u32[]{:S(2)}) copy-start(bf16[4,100,512]{2,1,0:T(8,128)(2,1)S(1)} %reshape.109) | copy-start | bytes 1228804
  117.1 58.8 %copy-start.6 = (f32[9775]{0:T(1024)S(1)}, f32[9775]{0:T(1024)}, u32[]{:S(2)}) copy-start(f32[9775]{0:T(1024)} %param.23) | copy-start | bytes 117304
  117.2 60.0 %copy-start.20 = (s32[5120]{0:T(1024)S(1)}, s32[5120]{0:T(1024)}, u32[]{:S(2)}) copy-start(s32[5120]{0:T(1024)} %param.18) | copy-start | bytes 61444
  309.8 51.4 %copy-start.4 = (f32[512,47]{0,1:T(8,128)S(1)}, f32[512,47]{0,1:T(8,128)}, u32[]{:S(2)}) copy-start(f32[512,47]{0,1:T(8,128)} %param.22) | copy-start | bytes 288772
  351.1 11.9 %copy-start.19 = (s32[5120]{0:T(1024)S(1)}, s32[5120]{0:T(1024)}, u32[]{:S(2)}) copy-start(s32[5120]{0:T(1024)} %param.19) | copy-start | bytes 61444
  382.8 384.9 %reduce-scatter.7.cloned.1.call-start = ((), (), s32[]{:S(2)}) async-start(), calls=%async_computation.5 | async-start | bytes 1081344
  422.6 11.1 %copy-start.21 = (f32[512]{0:T(512)}, f32[512]{0:T(512)S(1)}, u32[]{:S(2)}) copy-start(f32[512]{0:T(512)S(1)} %get-tuple-element.86) | copy-start | bytes 6148
  422.6 11.1 %copy-start.23 = (f32[512]{0:T(512)}, f32[512]{0:T(512)S(1)}, u32[]{:S(2)}) copy-start(f32[512]{0:T(512)S(1)} %get-tuple-element.85) | copy-start | bytes 6148
  433.7 109.1 %copy-start = (bf16[5120,512]{1,0:T(8,128)(2,1)}, bf16[5120,512]{1,0:T(8,128)(2,1)S(1)}, u32[]{:S(2)}) copy-start(bf16[5120,512]{1,0:T(8,128)(2,1)S(1)} %multiply_convert_fusion.1) | copy-start | bytes 15728644
  433.7 109.1 %copy-start.25 = (f32[512]{0:T(512)S(1)}, f32[512]{0:T(512)}, u32[]{:S(2)}) copy-start(f32[512]{0:T(512)} %get-tuple-element.78) | copy-start | bytes 6148
  433.7 109.1 %copy-start.26 = (f32[47]{0:T(128)S(1)}, f32[47]{0:T(128)}, u32[]{:S(2)}) copy-start(f32[47]{0:T(128)} %get-tuple-element.103) | copy-start | bytes 568
  433.8 150.5 %copy-start.16 = (f32[2048]{0:T(1024)S(1)}, f32[2048]{0:T(1024)}, u32[]{:S(2)}) copy-start(f32[2048]{0:T(1024)} %get-tuple-element.123) | copy-start | bytes 24580
  632.7 18.4 %copy-start.2 = (bf16[4,100,512]{2,1,0:T(8,128)(2,1)S(1)}, bf16[4,100,512]{2,1,0:T(8,128)(2,1)}, u32[]{:S(2)}) copy-start(bf16[4,100,512]{2,1,0:T(8,128)(2,1)} %copy-done.1) | copy-start | bytes 1228804
  632.7 274.7 %reduce-scatter.5.cloned.1.call-start = ((), (), s32[]{:S(2)}) async-start(), calls=%async_computation.3 | async-start | bytes 4325376 | tf_op jit(solution)/shard_map/reduce_scatter | solution.py:162
  662.5 9.6 %copy-start.24 = (f32[512]{0:T(512)S(1)}, f32[512]{0:T(512)}, u32[]{:S(2)}) copy-start(f32[512]{0:T(512)} %copy-done.23) | copy-start | bytes 6148
  662.5 9.6 %copy-start.22 = (f32[512]{0:T(512)S(1)}, f32[512]{0:T(512)}, u32[]{:S(2)}) copy-start(f32[512]{0:T(512)} %copy-done.21) | copy-start | bytes 6148
  662.5 9.6 %copy-start.7 = (f32[9775]{0:T(1024)S(1)}, f32[9775]{0:T(1024)}, u32[]{:S(2)}) copy-start(f32[9775]{0:T(1024)} %param.23) | copy-start | bytes 117304
  662.5 9.6 %copy-start.14 = (f32[9775]{0:T(1024)S(1)}, f32[9775]{0:T(1024)}, u32[]{:S(2)}) copy-start(f32[9775]{0:T(1024)} %param.31) | copy-start | bytes 117304
  662.5 9.6 %copy-start.15 = (f32[9775]{0:T(1024)S(1)}, f32[9775]{0:T(1024)}, u32[]{:S(2)}) copy-start(f32[9775]{0:T(1024)} %param.27) | copy-start | bytes 117304
  662.5 10.3 %copy-start.5 = (f32[512,47]{0,1:T(8,128)S(1)}, f32[512,47]{0,1:T(8,128)}, u32[]{:S(2)}) copy-start(f32[512,47]{0,1:T(8,128)} %param.22) | copy-start | bytes 288772
  662.5 10.3 %copy-start.11 = (f32[512,47]{0,1:T(8,128)S(1)}, f32[512,47]{0,1:T(8,128)}, u32[]{:S(2)}) copy-start(f32[512,47]{0,1:T(8,128)} %param.30) | copy-start | bytes 288772
  662.5 10.3 %copy-start.12 = (f32[512,47]{0,1:T(8,128)S(1)}, f32[512,47]{0,1:T(8,128)}, u32[]{:S(2)}) copy-start(f32[512,47]{0,1:T(8,128)} %param.26) | copy-start | bytes 288772
  662.5 105.2 %copy-start.10 = (f32[400,16]{0,1:T(8,128)S(1)}, f32[400,16]{0,1:T(8,128)}, u32[]{:S(2)}) copy-start(f32[400,16]{0,1:T(8,128)} %param.20) | copy-start | bytes 76804
  662.5 105.1 %copy-start.17 = (f32[400,16]{0,1:T(8,128)S(1)}, f32[400,16]{0,1:T(8,128)}, u32[]{:S(2)}) copy-start(f32[400,16]{0,1:T(8,128)} %param.28) | copy-start | bytes 76804
  662.5 105.1 %copy-start.18 = (f32[400,16]{0,1:T(8,128)S(1)}, f32[400,16]{0,1:T(8,128)}, u32[]{:S(2)}) copy-start(f32[400,16]{0,1:T(8,128)} %param.24) | copy-start | bytes 76804
  662.5 244.9 %copy-start.3 = (f32[2048,16]{0,1:T(8,128)S(1)}, f32[2048,16]{0,1:T(8,128)}, u32[]{:S(2)}) copy-start(f32[2048,16]{0,1:T(8,128)} %param.21) | copy-start | bytes 393220
  662.6 244.9 %copy-start.8 = (f32[2048,16]{0,1:T(8,128)S(1)}, f32[2048,16]{0,1:T(8,128)}, u32[]{:S(2)}) copy-start(f32[2048,16]{0,1:T(8,128)} %param.29) | copy-start | bytes 393220
  662.6 244.9 %copy-start.9 = (f32[2048,16]{0,1:T(8,128)S(1)}, f32[2048,16]{0,1:T(8,128)}, u32[]{:S(2)}) copy-start(f32[2048,16]{0,1:T(8,128)} %param.25) | copy-start | bytes 393220
  672.1 238.6 %copy-start.13 = (f32[9775]{0:T(1024)}, f32[9775]{0:T(1024)S(1)}, u32[]{:S(2)}) copy-start(f32[9775]{0:T(1024)S(1)} %constant_dynamic-update-slice_fusion) | copy-start | bytes 117304
Sparse Core Ops, SparseCore 0:
  11.5 59.5 all-gather.1
  382.9 120.7 all-reduce.4
  632.8 134.7 reduce-scatter.6
  770.5 136.9 reduce-scatter.4
where the time goes:
time: 924 us; the launch traced here: 918 us
  blocking collectives  285 us (31%)
  waiting for transfers between devices  232 us (25%)
  matrix products  209 us (23%)
  other arithmetic  158 us (17%)
  local copies, waits for them, and re-layouts  17.7 us (2%)
  between operations  15.4 us (2%)
    reduce_scatter x1, waiting for transfers between devices, local(): lax.psum_scatter(mid_part, 'shard', scatter_dimension=1, tiled=True)  138 us
    dot_general x1, matrix products, local(): jnp.dot(mid_grad_low, mid_full.T, preferred_element_type=jnp.float32)  109 us
    unnamed x5, waiting for transfers between devices  93.3 us
    psum x2, blocking collectives, moments(): lax.psum(jnp.sum(centered * centered * bucket[:, None], axis=0), 'shard')  82.5 us
    psum x2, blocking collectives, moments(): lax.psum((jnp.sum(masked, axis=0), jnp.sum(bucket)), 'shard')  76.6 us
    convert_element_type x1, other arithmetic, local(): concat_low = prelu_apply(branch_act, slope2).astype(jnp.bfloat16)  66.5 us
    all_gather x1, blocking collectives, local(): branch_full = lax.all_gather(branch_low, 'shard', axis=1, tiled=True)  44.7 us
    psum x1, blocking collectives, local(): lax.psum((slope_one_part, slope_two_part, jnp.sum(norm_grad * branch_hat...  41.4 us
  transfers between devices with their start and end apart: 4, of which 2 were waited for; matrix products, arithmetic and copies ran while one was open for 35% of the time, Pallas kernels for 0%

commit v1 on v0

--- a/solution.py
+++ b/solution.py
@@ -1,8 +1,11 @@
+import functools
 import math
 
 import jax
 import jax.numpy as jnp
 from jax import lax
+from jax.experimental import pallas as pl
+from jax.experimental.pallas import tpu as pltpu
 from jax.sharding import PartitionSpec as P
 
 K = 4
@@ -201,6 +204,912 @@
     )
 
 
+LOG2E = 1.4426950408889634
+LN2 = 0.6931471805599453
+LOW = jnp.bfloat16
+WIDE = jnp.float32
+FP = 128
+TILE = 256
+CHUNK = 32
+MESH = pl.DeviceIdType.MESH
+
+
+def soft_two(u):
+    return jnp.maximum(u, jnp.log2(1.0 + jnp.exp2(jnp.minimum(u, 126.0))))
+
+
+def dot_nn(a, b):
+    return jnp.dot(a, b, preferred_element_type=WIDE)
+
+
+def dot_nt(a, b):
+    return lax.dot_general(a, b, (((1,), (1,)), ((), ())), preferred_element_type=WIDE)
+
+
+def column(row):
+    return jnp.broadcast_to(row, (FP, FP)).T
+
+
+def split_three(v):
+    hi = v.astype(LOW)
+    rest = v - hi.astype(WIDE)
+    mid = rest.astype(LOW)
+    return hi, mid, (rest - mid.astype(WIDE)).astype(LOW)
+
+
+def fold_halves(v):
+    return v[:, :128] + v[:, 128:]
+
+
+def net_kernel(
+    nch,
+    count_ref,
+    feats_hbm,
+    code_ref,
+    wb_ref,
+    wm_ref,
+    wh_ref,
+    small_ref,
+    score_hbm,
+    part_hbm,
+    soft_hbm,
+    gm_out,
+    gb_out,
+    head_out,
+    rows_out,
+    corr_out,
+    xa,
+    cat,
+    mid_z,
+    dz,
+    cat_s,
+    soft_s,
+    pre_s,
+    wp,
+    cols,
+    wb_own,
+    wb_all,
+    wm_own,
+    wm_all,
+    gram,
+    gram_sib,
+    gram_in,
+    gram_all,
+    wbt,
+    wht,
+    whn,
+    small_t,
+    acc,
+    msg_own,
+    msg_sib,
+    msg_in,
+    bn2,
+    head_acc,
+    bias_acc,
+    head_loc,
+    head_sib,
+    head_in,
+    head_all,
+    pgrad,
+    pgrad_sib,
+    pgrad_in,
+    gm_in,
+    rows_own,
+    rows_all,
+    part_s,
+    score_s,
+    load_sem,
+    soft_sem,
+    part_sem,
+    score_sem,
+    send_sem,
+    recv_sem,
+):
+    nodes = feats_hbm.shape[1]
+    tiles = nodes // TILE
+    rb = wb_ref.shape[0]
+    hid = H
+    me = lax.axis_index("shard")
+    chip = me // 2
+    core = lax.rem(me, 2)
+    sibling = me + 1 - 2 * core
+    count = count_ref[0]
+
+    def peer(s):
+        return lax.rem(chip + s, nch) * 2 + core
+
+    def origin(s):
+        return lax.rem(chip + nch - s, nch)
+
+    def to_peer(i, s, src, dst):
+        return pltpu.make_async_remote_copy(
+            src_ref=src,
+            dst_ref=dst,
+            send_sem=send_sem.at[i, s],
+            recv_sem=recv_sem.at[i, s],
+            device_id=(peer(s),),
+            device_id_type=MESH,
+        )
+
+    def to_sibling(i, src, dst):
+        return pltpu.make_async_remote_copy(
+            src_ref=src,
+            dst_ref=dst,
+            send_sem=send_sem.at[i, 0],
+            recv_sem=recv_sem.at[i, 0],
+            device_id=(sibling,),
+            device_id_type=MESH,
+        )
+
+    def mask_row(start, width):
+        lane = lax.broadcasted_iota(jnp.int32, (1, width), 1) + start
+        return (lane < count).astype(WIDE)
+
+    load = pltpu.make_async_copy(feats_hbm, cat.at[pl.ds(0, K * F), :], load_sem.at[0])
+    load.start()
+
+    barrier = pltpu.get_barrier_semaphore()
+    for s in range(1, nch):
+        pl.semaphore_signal(barrier, inc=1, device_id=(peer(s),), device_id_type=MESH)
+    pl.semaphore_signal(barrier, inc=1, device_id=(sibling,), device_id_type=MESH)
+
+    wb_own[...] = jnp.zeros(wb_own.shape, LOW)
+    for k in range(K):
+        wb_own[k, :, 0:F] = wb_ref[:, k * F : (k + 1) * F].astype(LOW)
+    wm_own[...] = wm_ref[...].astype(LOW)
+    pl.semaphore_wait(barrier, nch)
+
+    def wb_slot(c):
+        return wb_all.at[:, c, core]
+
+    def wb_send(s):
+        return to_peer(0, s, wb_own, wb_slot(chip))
+
+    def wm_send(s):
+        return to_peer(1, s, wm_own, wm_all.at[chip, core])
+
+    for s in range(1, nch):
+        wb_send(s).start()
+    wb_all[:, chip, core] = wb_own[...]
+    wm_all[chip, core] = wm_own[...]
+
+    small_t[...] = jnp.concatenate(
+        [small_ref[...], jnp.zeros((FP - small_ref.shape[0], FP), WIDE)], axis=0
+    ).T
+
+    load.wait()
+    for s in range(1, nch):
+        wm_send(s).start()
+
+    width = 2 * TILE
+    row_id = lax.broadcasted_iota(jnp.int32, (112, width), 0)
+
+    def build(i, carry):
+        start = pl.multiple_of(i * width, width)
+        here = mask_row(start, width)
+        x = cat[0 : K * F + 16, pl.ds(start, width)].astype(WIDE)
+        for k in range(K):
+            piece = x[k * F : k * F + 112]
+            piece = jnp.where(row_id < F, piece * here, jnp.where(row_id < F + 3, here, 0.0))
+            xa[k, 0:112, pl.ds(start, width)] = piece.astype(LOW)
+            xa[k, 112:FP, pl.ds(start, width)] = jnp.zeros((FP - 112, width), LOW)
+        return carry
+
+    cat[K * F : K * F + 16, :] = jnp.zeros((16, nodes), LOW)
+    lax.fori_loop(0, nodes // width, build, 0)
+
+    rows_g = gram.shape[2]
+    for k in range(K):
+        g = dot_nt(xa[k], xa[k])
+        gram[pl.ds(k * nch // K, nch // K)] = g.reshape(nch // K, 2, rows_g, FP)
+
+    def reduce_one(i, own, sib):
+        to_sibling(i, own.at[:, 1 - core], sib).start()
+        to_sibling(i, own.at[:, 1 - core], sib).wait()
+
+    def reduce_two(i, own, sib, got):
+        own[:, core] = own[:, core] + sib[...]
+        for s in range(1, nch):
+            to_peer(i, s, own.at[lax.rem(chip + s, nch), core], got.at[chip]).start()
+        got[chip] = own[chip, core]
+
+    def reduce_wait(i, own, got):
+        for s in range(1, nch):
+            to_peer(i, s, own.at[lax.rem(chip + s, nch), core], got.at[chip]).wait_recv()
+        for s in range(1, nch):
+            to_peer(i, s, own.at[lax.rem(chip + s, nch), core], got.at[chip]).wait_send()
+
+    def total_of(got):
+        t = got[0].astype(WIDE)
+        for c in range(1, nch):
+            t = t + got[c].astype(WIDE)
+        return t
+
+    def spread_one(i, every):
+        for s in range(1, nch):
+            to_peer(i, s, every.at[chip, core], every.at[chip, core]).start()
+
+    def spread_two(i, every):
+        for s in range(1, nch):
+            to_peer(i, s, every.at[chip, core], every.at[chip, core]).wait()
+        to_sibling(i, every.at[:, core], every.at[:, core]).start()
+
+    def spread_wait(i, every):
+        to_sibling(i, every.at[:, core], every.at[:, core]).wait()
+
+    reduce_one(2, gram, gram_sib)
+    reduce_two(2, gram, gram_sib, gram_in)
+    for s in range(1, nch):
+        wb_send(s).wait()
+    to_sibling(0, wb_all.at[:, :, core], wb_all.at[:, :, core]).start()
+    reduce_wait(2, gram, gram_in)
+    gram_all[chip, core] = total_of(gram_in)
+    spread_one(3, gram_all)
+    wht[...] = jnp.zeros(wht.shape, LOW)
+    wht[0:C, :] = wh_ref[...].astype(LOW)
+    whn[...] = jnp.concatenate(
+        [wh_ref[...], jnp.zeros((FP - C, hid), WIDE)], axis=0
+    ).T.astype(LOW)
+    acc[...] = jnp.zeros(acc.shape, WIDE)
+    to_sibling(0, wb_all.at[:, :, core], wb_all.at[:, :, core]).wait()
+    for k in range(K):
+        wbt[k] = wb_all[k].reshape(hid, FP).astype(WIDE).T.astype(LOW)
+    spread_two(3, gram_all)
+    spread_wait(3, gram_all)
+
+    def branch_gram(k):
+        return gram_all[pl.ds(k * nch // K, nch // K)].reshape(FP, FP)
+
+    def branch_stats(w, g, g_parts):
+        filled = g[F : F + 1, F : F + 1]
+        wg = dot_nn(w, g_parts[0]) + dot_nn(w, g_parts[1]) + dot_nn(w, g_parts[2])
+        wf = w.astype(WIDE)
+        mean = wg[:, F : F + 1] / filled
+        second = jnp.sum(wg * wf, axis=1, keepdims=True) / filled
+        var = jnp.maximum(second - mean * mean, 0.0)
+        return wf, wg, mean, lax.rsqrt(var + EPS), filled
+
+    lane = lax.broadcasted_iota(jnp.int32, (FP, FP), 1)
+    blocks = hid // FP
+    for k in range(K):
+        g = branch_gram(k)
+        g_parts = split_three(g)
+        wk = wb_all[k].reshape(hid, FP)
+        for q in range(blocks):
+            w = wk[q * FP : (q + 1) * FP]
+            wf, wg, mean, inv, filled = branch_stats(w, g, g_parts)
+            c = k * blocks + q
+            gain = small_t[:, c : c + 1]
+            shift = small_t[:, K * blocks + c : K * blocks + c + 1]
+            slope1 = small_t[:, 2 * K * blocks + c : 2 * K * blocks + c + 1]
+            slope2 = small_t[:, 3 * K * blocks + c : 3 * K * blocks + c + 1]
+            ginv = gain * inv
+            scaled = wf * (-LOG2E * ginv)
+            hi = scaled.astype(LOW).astype(WIDE)
+            lo = scaled - hi
+            b1, b2, b3 = split_three(-LOG2E * (shift - ginv * mean))
+            hi = jnp.where(lane == F, b1.astype(WIDE), hi)
+            hi = jnp.where(lane == F + 1, b2.astype(WIDE), hi)
+            hi = jnp.where(lane == F + 2, b3.astype(WIDE), hi)
+            here = slice(q * FP, (q + 1) * FP)
+            wp[k, here, 0:FP] = hi.astype(LOW)
+            wp[k, here, FP : 2 * FP] = lo.astype(LOW)
+            there = slice(c * FP, (c + 1) * FP)
+            cols[0, there, :] = jnp.broadcast_to(1.0 - slope1, (FP, FP))
+            cols[1, there, :] = jnp.broadcast_to(1.0 - slope2, (FP, FP))
+            cols[2, there, :] = jnp.broadcast_to(ginv, (FP, FP))
+
+    for s in range(1, nch):
+        wm_send(s).wait()
+    to_sibling(1, wm_all.at[:, core], wm_all.at[:, core]).start()
+    to_sibling(1, wm_all.at[:, core], wm_all.at[:, core]).wait()
+
+    def branch_dot(k, j):
+        x = xa[k, :, pl.ds(pl.multiple_of(j * TILE, TILE), TILE)]
+        pre_s[k % 2] = dot_nn(wp[k], jnp.concatenate([x, x], axis=0))
+
+    def mid_dot(k, slot, start):
+        w = wm_all[:, :, :, k * hid : (k + 1) * hid].reshape(hid, hid)
+        d = dot_nn(w, cat_s[slot, k * hid : (k + 1) * hid, :])
+        if k == 0:
+            mid_z[:, pl.ds(start, TILE)] = d
+            return
+        z = mid_z[:, pl.ds(start, TILE)] + d
+        mid_z[:, pl.ds(start, TILE)] = z
+        if k == K - 1:
+            masked = z * mask_row(start, TILE)
+            acc[0] += fold_halves(masked)
+            acc[1] += fold_halves(masked * z)
+
+    def forward_chunk(k, r, slot, start):
+        rows = slice(k * hid + r, k * hid + r + CHUNK)
+        for half in range(2):
+            lanes = slice(half * 128, half * 128 + 128)
+            u1 = pre_s[k % 2, r : r + CHUNK, lanes]
+            m1 = soft_two(u1)
+            u2 = u1 - cols[0, rows, :] * m1
+            m2 = soft_two(u2)
+            v = ((u2 - cols[1, rows, :] * m2) * -LN2).astype(LOW)
+            cat_s[slot, rows, lanes] = v
+            cat[rows, pl.ds(start + half * 128, 128)] = v
+            soft_s[slot, 0, rows, lanes] = m1.astype(LOW)
+            soft_s[slot, 1, rows, lanes] = m2.astype(LOW)
+
+    def soft_save(slot, j):
+        return pltpu.make_async_copy(soft_s.at[slot], soft_hbm.at[j], soft_sem.at[slot])
+
+    cat_s[1] = jnp.zeros(cat_s.shape[1:], LOW)
+    branch_dot(0, 0)
+
+    def forward(i, carry):
+        for slot in range(2):
+            j = i * 2 + slot
+
+            @pl.when(i > 0)
+            def _():
+                soft_save(slot, j - 2).wait()
+
+            start = pl.multiple_of(j * TILE, TILE)
+            before = pl.multiple_of(jnp.maximum(j - 1, 0) * TILE, TILE)
+            for k in range(K):
+                mid_dot(k, 1 - slot, before)
+                if k < K - 1:
+                    branch_dot(k + 1, j)
+                else:
+                    branch_dot(0, jnp.minimum(j + 1, tiles - 1))
+                for r in range(0, hid, CHUNK):
+                    forward_chunk(k, r, slot, start)
+            soft_save(slot, j).start()
+        return carry
+
+    lax.fori_loop(0, tiles // 2, forward, 0)
+    for k in range(K):
+        mid_dot(k, 1, (tiles - 1) * TILE)
+    for slot in range(2):
+        soft_save(slot, tiles - 2 + slot).wait()
+
+    def rows_of(i):
+        return jnp.sum(acc[i].T, axis=0, keepdims=True)
+
+    def share_start(n, i):
+        to_sibling(i, msg_own.at[n], msg_sib.at[n]).start()
+
+    def share_mid(n, i):
+        to_sibling(i, msg_own.at[n], msg_sib.at[n]).wait()
+        msg_in[n, chip] = msg_own[n] + msg_sib[n]
+        for s in range(1, nch):
+            to_peer(i, s, msg_in.at[n, chip], msg_in.at[n, chip]).start()
+
+    def share_end(n, i):
+        for s in range(1, nch):
+            to_peer(i, s, msg_in.at[n, chip], msg_in.at[n, chip]).wait()
+        return total_of(msg_in.at[n])
+
+    def put_rows(n, first, row):
+        for q in range(blocks):
+            msg_own[n, first + q : first + q + 1, :] = row[:, q * FP : (q + 1) * FP]
+
+    put_rows(0, 0, rows_of(0))
+    put_rows(0, blocks, rows_of(1))
+    share_start(0, 4)
+    share_mid(0, 4)
+    for r in range(0, K * hid, FP):
+        rows = slice(r, r + FP)
+        c1 = cols[0, rows, :]
+        ginv = cols[2, rows, :]
+        cols[0, rows, :] = ginv * (1.0 - c1)
+        cols[2, rows, :] = ginv * c1
+    for q in range(4):
+        w = wm_all[q * nch // 4 : (q + 1) * nch // 4].reshape(FP, 2048)
+        w = w.T
+        cat_s[q // 2, :, (q % 2) * FP : (q % 2 + 1) * FP] = w
+    head_acc[...] = jnp.zeros(head_acc.shape, WIDE)
+    bias_acc[...] = jnp.zeros(bias_acc.shape, WIDE)
+    acc[...] = jnp.zeros(acc.shape, WIDE)
+    tot = share_end(0, 4)
+    filled = branch_gram(0)[F : F + 1, F : F + 1]
+
+    base = 4 * K * blocks
+    means = []
+    for q in range(blocks):
+        here = slice(q * FP, (q + 1) * FP)
+        gain = small_ref[base + q : base + q + 1, :]
+        shift = small_ref[base + blocks + q : base + blocks + q + 1, :]
+        slope3 = small_ref[base + 2 * blocks + q : base + 2 * blocks + q + 1, :]
+        mean = tot[q : q + 1] / filled
+        var = jnp.maximum(tot[blocks + q : blocks + q + 1] / filled - mean * mean, 0.0)
+        inv = lax.rsqrt(var + EPS)
+        means.append((mean, inv, gain))
+        bn2[0, here, :] = column(-LOG2E * gain * inv)
+        bn2[1, here, :] = column(-LOG2E * (shift - gain * inv * mean))
+        bn2[2, here, :] = column(mean)
+        bn2[3, here, :] = column(1.0 - slope3)
+
+    bias_col = small_t[0 : 48, base + 3 * blocks : base + 3 * blocks + 1]
+    class_id = lax.broadcasted_iota(jnp.int32, (48, TILE), 0)
+
+    def score_save(slot, j):
+        return pltpu.make_async_copy(
+            score_s.at[slot],
+            score_hbm.at[:, pl.ds(pl.multiple_of(j * TILE, TILE), TILE)],
+            score_sem.at[slot],
+        )
+
+    def head(i, carry):
+        for slot in range(2):
+            j = i * 2 + slot
+
+            @pl.when(i > 0)
+            def _():
+                score_save(slot, j - 2).wait()
+
+            start = pl.multiple_of(j * TILE, TILE)
+            here = mask_row(start, TILE)
+            for r in range(0, hid, CHUNK):
+                rows = slice(r, r + CHUNK)
+                for half in range(2):
+                    lanes = slice(half * 128, half * 128 + 128)
+                    z = mid_z[rows, pl.ds(start + half * 128, 128)]
+                    u = z * bn2[0, rows, :] + bn2[1, rows, :]
+                    m = soft_two(u)
+                    v = (u - bn2[3, rows, :] * m) * -LN2
+                    soft_s[0, 0, rows, lanes] = v.astype(LOW)
+                    pre_s[0, rows, lanes] = m
+            s = dot_nn(wht[...], soft_s[0, 0, 0:hid, :]) + bias_col
+            score_s[slot] = s * here
+            s = jnp.where(class_id < C, s, -1e30)
+            e = jnp.exp(s - jnp.max(s, axis=0, keepdims=True))
+            p = e / jnp.sum(e, axis=0, keepdims=True)
+            code = code_ref[:, pl.ds(start, TILE)]
+            trained = here * (code >= 0).astype(WIDE)
+            hot = (class_id == code).astype(WIDE)
+            g = ((p - hot) * trained).astype(LOW)
+            bias_acc[...] += fold_halves(g.astype(WIDE))
+            head_acc[...] += dot_nt(g, soft_s[0, 0, 0:hid, :])
+            pre_s[1] = dot_nn(whn[:, 0:48], g)
+            for r in range(0, hid, CHUNK):
+                rows = slice(r, r + CHUNK)
+                sums = [0.0, 0.0, 0.0]
+                for half in range(2):
+                    lanes = slice(half * 128, half * 128 + 128)
+                    d = pre_s[1, rows, lanes]
+                    m = pre_s[0, rows, lanes]
+                    c3 = bn2[3, rows, :]
+                    dy = d * ((1.0 - c3) + c3 * jnp.exp2(-m))
+                    z = mid_z[rows, pl.ds(start + half * 128, 128)] - bn2[2, rows, :]
+                    sums[0] += d * m
+                    sums[1] += dy
+                    sums[2] += dy * z
+                    dz[rows, pl.ds(start + half * 128, 128)] = dy.astype(LOW)
+                for q in range(3):
+                    acc[q, rows, :] += sums[q]
+            score_save(slot, j).start()
+        return carry
+
+    lax.fori_loop(0, tiles // 2, head, 0)
+    for slot in range(2):
+        score_save(slot, tiles - 2 + slot).wait()
+
+    put_rows(1, 0, rows_of(1))
+    put_rows(1, blocks, rows_of(2))
+    share_start(1, 5)
+    share_mid(1, 5)
+    flat = jnp.concatenate(
+        [head_acc[:, q * FP : (q + 1) * FP] for q in range(blocks)]
+        + [
+            jnp.concatenate(
+                [bias_acc[...], jnp.zeros((FP - 48, FP), WIDE)], axis=0
+            ).T.sum(axis=0, keepdims=True).reshape(1, FP),
+            jnp.zeros((7, FP), WIDE),
+        ],
+        axis=0,
+    )
+    rows_h = head_loc.shape[2]
+    slope_row = rows_of(0) * -LN2
+    flat = jnp.concatenate(
+        [flat]
+        + [slope_row[:, q * FP : (q + 1) * FP] for q in range(blocks)]
+        + [jnp.zeros((2 * nch * rows_h - 200 - blocks, FP), WIDE)],
+        axis=0,
+    )
+    head_loc[...] = flat.reshape(nch, 2, rows_h, FP)
+    to_sibling(6, head_loc.at[:, 1 - core], head_sib).start()
+    tot = share_end(1, 5)
+
+    for q in range(blocks):
+        here = slice(q * FP, (q + 1) * FP)
+        mean, inv, gain = means[q]
+        grad_shift = tot[q : q + 1]
+        grad_gain = tot[blocks + q : blocks + q + 1] * inv
+        a = gain * inv
+        slope = a * grad_gain * inv / filled
+        bn2[0, here, :] = column(a)
+        bn2[1, here, :] = column(slope)
+        bn2[2, here, :] = column(a * grad_shift / filled - slope * mean)
+        msg_own[0, q : q + 1, :] = grad_gain
+        msg_own[0, blocks + q : blocks + q + 1, :] = grad_shift
+
+    def mid_back(j, carry):
+        start = pl.multiple_of(j * TILE, TILE)
+        here = mask_row(start, TILE)
+        for r in range(0, hid, CHUNK):
+            rows = slice(r, r + CHUNK)
+            for half in range(2):
+                at = pl.ds(start + half * 128, 128)
+                d = dz[rows, at].astype(WIDE) * bn2[0, rows, :]
+                t = mid_z[rows, at] * bn2[1, rows, :] + bn2[2, rows, :]
+                dz[rows, at] = (d - t * here[:, half * 128 : half * 128 + 128]).astype(LOW)
+        return carry
+
+    lax.fori_loop(0, tiles, mid_back, 0)
+
+    to_sibling(6, head_loc.at[:, 1 - core], head_sib).wait()
+    reduce_two(6, head_loc, head_sib, head_in)
+
+    def mid_grad(i, carry):
+        at = pl.multiple_of(i * TILE, TILE)
+        mid_z[:, pl.ds(at, TILE)] = dot_nt(dz[...], cat[pl.ds(at, TILE), :])
+        return carry
+
+    lax.fori_loop(0, K * hid // TILE, mid_grad, 0)
+    width_m = K * hid
+
+    for c in range(nch):
+        for e in range(2):
+            at = (2 * c + e) * rb
+
+            @pl.when(core != e)
+            def _():
+                wm_all[c, 0] = mid_z[at : at + rb, 0:width_m].astype(LOW)
+
+    to_sibling(8, wm_all.at[:, 0], wm_all.at[:, 1]).start()
+    reduce_wait(6, head_loc, head_in)
+    head_all[chip, core] = total_of(head_in)
+    spread_one(7, head_all)
+
+    def soft_load(slot, k, j):
+        return pltpu.make_async_copy(
+            soft_hbm.at[j, :, pl.ds(k * hid, hid), :],
+            soft_s.at[slot, :, pl.ds(0, hid), :],
+            soft_sem.at[slot],
+        )
+
+    def part_save(slot, k, j):
+        return pltpu.make_async_copy(
+            part_s.at[slot],
+            part_hbm.at[k, :, pl.ds(pl.multiple_of(j * TILE, TILE), TILE)],
+            part_sem.at[slot],
+        )
+
+    def back_dot(k, j, slot):
+        w = jnp.concatenate(
+            [cat_s[0, k * hid : (k + 1) * hid, :], cat_s[1, k * hid : (k + 1) * hid, :]], axis=1
+        )
+        pre_s[slot] = dot_nn(w, dz[:, pl.ds(pl.multiple_of(j * TILE, TILE), TILE)])
+
+    def tail_dots(k, j, slot):
+        t = soft_s[slot, 0, hid : 2 * hid, :]
+        x = xa[k, :, pl.ds(pl.multiple_of(j * TILE, TILE), TILE)]
+        acc[2] += dot_nt(t, x)
+        part_s[slot] = dot_nn(wbt[k, 0 : part_s.shape[1], :], t).astype(LOW)
+
+    for k in range(K):
+        acc[0] = jnp.zeros(acc.shape[1:], WIDE)
+        acc[1] = jnp.zeros(acc.shape[1:], WIDE)
+        acc[2] = jnp.zeros(acc.shape[1:], WIDE)
+        for slot in range(2):
+            soft_load(slot, k, slot).start()
+        back_dot(k, 0, 0)
+
+        def backward(i, carry):
+            for slot in range(2):
+                j = i * 2 + slot
+                soft_load(slot, k, j).wait()
+
+                @pl.when(i > 0)
+                def _():
+                    part_save(slot, k, j - 2).wait()
+
+                back_dot(k, jnp.minimum(j + 1, tiles - 1), 1 - slot)
+                for r in range(0, hid, CHUNK):
+                    rows = slice(r, r + CHUNK)
+                    wide_rows = slice(k * hid + r, k * hid + r + CHUNK)
+                    sums = [0.0, 0.0]
+                    for half in range(2):
+                        lanes = slice(half * 128, half * 128 + 128)
+                        d = pre_s[slot, rows, lanes]
+                        m1 = soft_s[slot, 0, rows, lanes].astype(WIDE)
+                        m2 = soft_s[slot, 1, rows, lanes].astype(WIDE)
+                        c2 = cols[1, wide_rows, :]
+                        da = d * ((1.0 - c2) + c2 * jnp.exp2(-m2))
+                        t = da * (cols[0, wide_rows, :] + cols[2, wide_rows, :] * jnp.exp2(-m1))
+                        sums[0] += d * m2
+                        sums[1] += da * m1
+                        soft_s[slot, 0, hid + r : hid + r + CHUNK, lanes] = t.astype(LOW)
+                    acc[0, rows, :] += sums[0]
+                    acc[1, rows, :] += sums[1]
+                tail_dots(k, j, slot)
+                part_save(slot, k, j).start()
+
+                @pl.when(i < tiles // 2 - 1)
+                def _():
+                    soft_load(slot, k, j + 2).start()
+            return carry
+
+        lax.fori_loop(0, tiles // 2, backward, 0)
+        for slot in range(2):
+            part_save(slot, k, tiles - 2 + slot).wait()
+
+        two = lax.broadcasted_iota(jnp.int32, (hid, FP), 1)
+        sl2 = jnp.sum(acc[0], axis=1, keepdims=True) * -LN2
+        sl1 = jnp.sum(acc[1], axis=1, keepdims=True) * -LN2
+        p = jnp.where(two == F + 4, sl1, jnp.where(two == F + 5, sl2, acc[2]))
+        if k > 1:
+            reduce_wait(9 + k - 2, pgrad.at[k % 2], pgrad_in.at[k - 2])
+        pgrad[k % 2] = p.reshape(nch, 2, rb, FP)
+        to_sibling(9 + k, pgrad.at[k % 2, :, 1 - core], pgrad_sib.at[k]).start()
+
+        if k == 0:
+            to_sibling(8, wm_all.at[:, 0], wm_all.at[:, 1]).wait()
+            for c in range(nch):
+                for e in range(2):
+                    at = (2 * c + e) * rb
+
+                    @pl.when(core == e)
+                    def _():
+                        v = mid_z[at : at + rb, 0:width_m] + wm_all[c, 1].astype(WIDE)
+                        wm_all[c, 0] = v.astype(LOW)
+
+            for s in range(1, nch):
+                to_peer(8, s, wm_all.at[lax.rem(chip + s, nch), 0], gm_in.at[chip]).start()
+            gm_in[chip] = wm_all[chip, 0]
+            spread_two(7, head_all)
+        if k == 1:
+            spread_wait(7, head_all)
+        if k > 0:
+            to_sibling(9 + k - 1, pgrad.at[(k - 1) % 2, :, 1 - core], pgrad_sib.at[k - 1]).wait()
+            reduce_two(9 + k - 1, pgrad.at[(k - 1) % 2], pgrad_sib.at[k - 1], pgrad_in.at[k - 1])
+
+    k = K - 1
+    to_sibling(9 + k, pgrad.at[k % 2, :, 1 - core], pgrad_sib.at[k]).wait()
+    reduce_two(9 + k, pgrad.at[k % 2], pgrad_sib.at[k], pgrad_in.at[k])
+    for s in range(1, nch):
+        to_peer(8, s, wm_all.at[lax.rem(chip + s, nch), 0], gm_in.at[chip]).wait()
+    gm_out[...] = total_of(gm_in)
+    for k in range(K - 2, K):
+        reduce_wait(9 + k, pgrad.at[k % 2], pgrad_in.at[k])
+
+    lane_s = lax.broadcasted_iota(jnp.int32, (rb, FP), 1)
+    quant = []
+    for k in range(K):
+        g = branch_gram(k)
+        w = wb_own[k]
+        wf, wg, mean, inv, filled = branch_stats(w, g, split_three(g))
+        p = total_of(pgrad_in.at[k])
+        st = p[:, F : F + 1]
+        tz = jnp.sum(jnp.where(lane_s < F, p * wf, 0.0), axis=1, keepdims=True)
+        gt = (tz - mean * st) * inv
+        totals = g[F : F + 1, :]
+        gb_out[k] = p - (st * totals + gt * inv * (wg - mean * totals)) / filled
+        q0 = gt * inv / filled
+        q1 = st / filled - q0 * mean
+        vals = [st, gt, p[:, F + 4 : F + 5], p[:, F + 5 : F + 6], q0, q1, inv]
+        block = jnp.zeros((rb, FP), WIDE)
+        for n, v in enumerate(vals):
+            block = jnp.where(lane_s == n, v, block)
+        quant.append(block)
+    quant = jnp.concatenate(quant + [jnp.zeros((FP - K * rb, FP), WIDE)], axis=0).T
+    rows_own[...] = quant[0:8, :]
+    rows_all[chip, core] = rows_own[...]
+    spread_one(13, rows_all)
+    spread_two(13, rows_all)
+    spread_wait(13, rows_all)
+    full = []
+    per = FP // rb
+    lane8 = lax.broadcasted_iota(jnp.int32, (8, FP), 1)
+    for k in range(K):
+        for t in range(hid // FP):
+            v = jnp.zeros((8, FP), WIDE)
+            for n in range(per):
+                d = t * per + n
+                piece = rows_all[d // 2, d % 2]
+                moved = pltpu.roll(piece, (n * rb - k * rb) % FP, 1)
+                v = jnp.where((lane8 >= n * rb) & (lane8 < (n + 1) * rb), moved, v)
+            full.append(v)
+    for c in range(K * blocks):
+        v = full[c]
+        gain = small_ref[c : c + 1, :]
+        unit = gain * v[6:7]
+        rows_out[c : c + 1, :] = v[1:2] / unit
+        rows_out[K * blocks + c : K * blocks + c + 1, :] = v[0:1] / unit
+        rows_out[2 * K * blocks + c : 2 * K * blocks + c + 1, :] = v[2:3]
+        rows_out[3 * K * blocks + c : 3 * K * blocks + c + 1, :] = v[3:4]
+    rows_out[base : base + 2 * blocks, :] = msg_own[0, 0 : 2 * blocks, :]
+    head_flat = head_all[...].reshape(2 * nch * rows_h, FP)
+    rows_out[base + 2 * blocks : base + 3 * blocks, :] = head_flat[200 : 200 + blocks]
+    rows_out[base + 3 * blocks : base + 3 * blocks + 1, :] = head_flat[192:193]
+    rows_out[base + 3 * blocks + 1 :, :] = jnp.zeros(
+        (rows_out.shape[0] - base - 3 * blocks - 1, FP), WIDE
+    )
+    for q in range(blocks):
+        head_out[:, q * FP : (q + 1) * FP] = head_flat[q * 48 : q * 48 + 48]
+    for k in range(K):
+        wt = wbt[k].astype(WIDE)
+        r0 = jnp.concatenate([full[k * blocks + q][4:5] for q in range(blocks)], axis=1)
+        r1 = jnp.concatenate([full[k * blocks + q][5:6] for q in range(blocks)], axis=1)
+        m = dot_nn((wt * r0).astype(LOW), wb_all[k].reshape(hid, FP))
+        v = jnp.sum(wt * r1, axis=1, keepdims=True)
+        corr_out[k] = jnp.where(lane == F, v, m).astype(LOW)
+
+
+def finish_kernel(count_ref, feats_ref, part_ref, corr_ref, score_ref, grad_ref, logit_ref):
+    width = feats_ref.shape[1]
+    lane = lax.broadcasted_iota(jnp.int32, (1, width), 1) + pl.program_id(0) * width
+    here = (lane < count_ref[0]).astype(WIDE)
+    row_id = lax.broadcasted_iota(jnp.int32, (112, width), 0)
+    x = feats_ref[...].astype(WIDE)
+    x = jnp.concatenate([x, jnp.zeros((16, width), WIDE)], axis=0)
+    for k in range(K):
+        piece = x[k * F : k * F + 112]
+        piece = jnp.where(row_id < F, piece * here, jnp.where(row_id < F + 1, here, 0.0))
+        fix = dot_nn(corr_ref[k, 0:112, 0:112], piece.astype(LOW))
+        out = part_ref[k].astype(WIDE) - fix
+        grad_ref[k * F : (k + 1) * F, :] = out[0:F]
+    logit_ref[...] = score_ref[0:C, :]
+
+
+def fused(
+    features,
+    counts,
+    labelled,
+    labels,
+    w_branch,
+    w_mid,
+    w_head,
+    small_params,
+    mom_branch,
+    mom_mid,
+    mom_head,
+    mom_small,
+    avg_branch,
+    avg_mid,
+    avg_head,
+    avg_small,
+):
+    nodes = features.shape[0]
+    devices = lax.axis_size("shard")
+    nch = devices // 2
+    rb = w_mid.shape[1]
+    tiles = nodes // TILE
+    rows_g = K * FP // devices
+    rows_h = 8
+    feats = features.T
+    code = jnp.where(labelled > 0, labels, -1).reshape(1, nodes)
+    small_rows = -(-small_params.shape[0] // (8 * FP)) * 8
+    small = jnp.pad(small_params, (0, small_rows * FP - small_params.shape[0])).reshape(
+        small_rows, FP
+    )
+    vmem = pl.BlockSpec(memory_space=pltpu.VMEM)
+    hbm = pl.BlockSpec(memory_space=pl.ANY)
+    smem = pl.BlockSpec(memory_space=pltpu.SMEM)
+    width_m = K * H
+    scores, part, soft, gm, gb, gh, gs, corr = pl.pallas_call(
+        functools.partial(net_kernel, nch),
+        out_shape=(
+            jax.ShapeDtypeStruct((48, nodes), WIDE),
+            jax.ShapeDtypeStruct((K, 112, nodes), LOW),
+            jax.ShapeDtypeStruct((tiles, 2, width_m, TILE), LOW),
+            jax.ShapeDtypeStruct((rb, width_m), WIDE),
+            jax.ShapeDtypeStruct((K, rb, FP), WIDE),
+            jax.ShapeDtypeStruct((48, H), WIDE),
+            jax.ShapeDtypeStruct((small_rows, FP), WIDE),
+            jax.ShapeDtypeStruct((K, FP, FP), LOW),
+        ),
+        in_specs=[smem, hbm] + [vmem] * 5,
+        out_specs=(hbm, hbm, hbm, vmem, vmem, vmem, vmem, vmem),
+        scratch_shapes=[
+            pltpu.VMEM((K, FP, nodes), LOW),
+            pltpu.VMEM((width_m, nodes), LOW),
+            pltpu.VMEM((H, nodes), WIDE),
+            pltpu.VMEM((H, nodes), LOW),
+            pltpu.VMEM((2, width_m, TILE), LOW),
+            pltpu.VMEM((2, 2, width_m, TILE), LOW),
+            pltpu.VMEM((2, H, TILE), WIDE),
+            pltpu.VMEM((K, H, 2 * FP), LOW),
+            pltpu.VMEM((3, width_m, FP), WIDE),
+            pltpu.VMEM((K, rb, FP), LOW),
+            pltpu.VMEM((K, nch, 2, rb, FP), LOW),
+            pltpu.VMEM((rb, width_m), LOW),
+            pltpu.VMEM((nch, 2, rb, width_m), LOW),
+            pltpu.VMEM((nch, 2, rows_g, FP), WIDE),
+            pltpu.VMEM((nch, rows_g, FP), WIDE),
+            pltpu.VMEM((nch, rows_g, FP), WIDE),
+            pltpu.VMEM((nch, 2, rows_g, FP), WIDE),
+            pltpu.VMEM((K, FP, H), LOW),
+            pltpu.VMEM((48, H), LOW),
+            pltpu.VMEM((H, FP), LOW),
+            pltpu.VMEM((FP, FP), WIDE),
+            pltpu.VMEM((3, H, FP), WIDE),
+            pltpu.VMEM((2, 8, FP), WIDE),
+            pltpu.VMEM((2, 8, FP), WIDE),
+            pltpu.VMEM((2, nch, 8, FP), WIDE),
+            pltpu.VMEM((4, H, FP), WIDE),
+            pltpu.VMEM((48, H), WIDE),
+            pltpu.VMEM((48, FP), WIDE),
+            pltpu.VMEM((nch, 2, rows_h, FP), WIDE),
+            pltpu.VMEM((nch, rows_h, FP), WIDE),
+            pltpu.VMEM((nch, rows_h, FP), WIDE),
+            pltpu.VMEM((nch, 2, rows_h, FP), WIDE),
+            pltpu.VMEM((2, nch, 2, rb, FP), WIDE),
+            pltpu.VMEM((K, nch, rb, FP), WIDE),
+            pltpu.VMEM((K, nch, rb, FP), WIDE),
+            pltpu.VMEM((nch, rb, width_m), LOW),
+            pltpu.VMEM((8, FP), WIDE),
+            pltpu.VMEM((nch, 2, 8, FP), WIDE),
+            pltpu.VMEM((2, 112, TILE), LOW),
+            pltpu.VMEM((2, 48, TILE), WIDE),
+            pltpu.SemaphoreType.DMA((1,)),
+            pltpu.SemaphoreType.DMA((2,)),
+            pltpu.SemaphoreType.DMA((2,)),
+            pltpu.SemaphoreType.DMA((2,)),
+            pltpu.SemaphoreType.DMA((14, nch)),
+            pltpu.SemaphoreType.DMA((14, nch)),
+        ],
+        compiler_params=pltpu.CompilerParams(
+            collective_id=0, has_side_effects=True, vmem_limit_bytes=65400 * 1024
+        ),
+    )(counts, feats, code, w_branch.T, w_mid.T, w_head.T, small)
+    step = 512
+    fgrad, logits = pl.pallas_call(
+        finish_kernel,
+        grid=(nodes // step,),
+        out_shape=(
+            jax.ShapeDtypeStruct((K * F, nodes), WIDE),
+            jax.ShapeDtypeStruct((C, nodes), WIDE),
+        ),
+        in_specs=[
+            smem,
+            pl.BlockSpec((K * F, step), lambda i: (0, i)),
+            pl.BlockSpec((K, 112, step), lambda i: (0, 0, i)),
+            pl.BlockSpec((K, FP, FP), lambda i: (0, 0, 0)),
+            pl.BlockSpec((48, step), lambda i: (0, i)),
+        ],
+        out_specs=(
+            pl.BlockSpec((K * F, step), lambda i: (0, i)),
+            pl.BlockSpec((C, step), lambda i: (0, i)),
+        ),
+    )(counts, feats, part, corr, scores)
+    root = math.sqrt(nodes * devices)
+    grad_branch = jnp.concatenate([gb[k, :, :F] for k in range(K)], axis=1).T
+    grad_mid = gm.T
+    grad_head = gh[:C].T
+    grad_small = gs.reshape(-1)[: small_params.shape[0]]
+    mom_b, avg_b, new_b = nesterov(w_branch, grad_branch, mom_branch, avg_branch, 0.8 / root)
+    mom_m, avg_m, new_m = nesterov(w_mid, grad_mid, mom_mid, avg_mid, 0.08 / root)
+    mom_h, avg_h, new_h = nesterov(w_head, grad_head, mom_head, avg_head, 0.3 / root)
+    mom_s, avg_s, new_s = nesterov(small_params, grad_small, mom_small, avg_small, 1.0 / root)
+    return (
+        logits.T,
+        fgrad.T,
+        grad_branch,
+        grad_mid,
+        grad_head,
+        grad_small,
+        mom_b,
+        mom_m,
+        mom_h,
+        mom_s,
+        avg_b,
+        avg_m,
+        avg_h,
+        avg_s,
+        new_b,
+        new_m,
+        new_h,
+        new_s,
+    )
+
+
 def solution(mesh):
     in_specs = (
         P("shard", None),
@@ -240,4 +1149,5 @@
         P(),
         P(),
     )
-    return jax.shard_map(local, mesh=mesh, in_specs=in_specs, out_specs=out_specs, check_vma=False)
+    run = fused if H % (16 * mesh.size) == 0 else local
+    return jax.shard_map(run, mesh=mesh, in_specs=in_specs, out_specs=out_specs, check_vma=False)

time: 924 us -> 263 us (0.28)
  blocking collectives: 285 us -> 0 us
  Pallas kernels: 0 us -> 249 us
  waiting for transfers between devices: 232 us -> 0 us
  matrix products: 209 us -> 0 us
  other arithmetic: 158 us -> 8.04 us
  local copies, waits for them, and re-layouts: 17.7 us -> 2.85 us
  between operations: 15.4 us -> 1.32 us
    pallas_call x0 -> x2, Pallas kernels: none -> 249 us  [the longest x1 237 us: fused(): pl.pallas_call(functools.partial(net_kernel, nch), out_shape=(jax.ShapeDt...]
    psum x6 -> x0, blocking collectives: 240 us -> none  [the longest x2 82.5 us: moments(): lax.psum(jnp.sum(centered * centered * bucket[:, None], axis=0), 'shard')]
    dot_general x9 -> x0, matrix products: 209 us -> none  [the longest x1 109 us: local(): jnp.dot(mid_grad_low, mid_full.T, preferred_element_type=jnp.float32)]
    reduce_scatter x1 -> x0, waiting for transfers between devices: 138 us -> none  [local(): lax.psum_scatter(mid_part, 'shard', scatter_dimension=1, tiled=True)]
    convert_element_type x7 -> x0, other arithmetic: 125 us -> none  [the longest x1 66.5 us: local(): concat_low = prelu_apply(branch_act, slope2).astype(jnp.bfloat16)]
    unnamed x5 -> x0, waiting for transfers between devices: 93.3 us -> none
    all_gather x1 -> x0, blocking collectives: 44.7 us -> none  [local(): branch_full = lax.all_gather(branch_low, 'shard', axis=1, tiled=True)]
    reduce_sum x5 -> x0, other arithmetic: 25 us -> none  [the longest x2 22.4 us: moments(): jnp.sum(centered * centered * bucket[:, None], axis=0)]
  transfers between devices with their start and end apart: 4 -> 0, of which waited for: 2 -> 0; matrix products, arithmetic and copies ran while one was open for 35% -> 0% of each run, Pallas kernels for 0% -> 0%
where the time goes in v1:
time: 263 us; the launch traced here: 261 us
  Pallas kernels  249 us (95%)
  other arithmetic  8.04 us (3%)
  local copies, waits for them, and re-layouts  2.85 us (1%)
    pallas_call x1, Pallas kernels, fused(): pl.pallas_call(functools.partial(net_kernel, nch), out_shape=(jax.ShapeDt...  237 us
    pallas_call x1, Pallas kernels, fused(): pl.pallas_call(finish_kernel, grid=(nodes // step,), out_shape=(jax.Shape...  11.3 us
    add x4, other arithmetic, nesterov(): average_new = DECAY * average_old + (1.0 - DECAY) * weight_new  6.69 us

profile of v1, /device:TPU:0, one launch (start us, length us, event | category | flops | bytes accessed | tf_op | source)
XLA Modules:
  0.0 260.8 jit_solution(15857197774046866452)
XLA Ops:
  1.3 1.4 compare_select_fusion
  2.7 1.4 pad_bitcast_fusion.small_ref
  4.1 237.3 %shard_map.295 = (f32[48,5120]{1,0:T(8,128)}, bf16[4,112,5120]{2,1,0:T(8,128)(2,1)}, bf16[20,2,2048,256]{3,2,1,0:T(8,128)(2,1)}, f32[16,2048]{1,0:T(8,128)}, f32...) custom-call(s32[1]{0:T(128)S(6)} %copy.35.count_ref, ...), custom_call_target="tpu_custom_call" | custom-call | tf_op jit(solution)/shard_map/pallas_call | solution.py:996
  241.4 0.0 copy-start
  241.4 0.8 slice_bitcast_fusion.4
  242.2 1.5 multiply_add_fusion.6
  243.7 1.5 multiply_add_fusion.4
  245.2 1.8 multiply_add_fusion.2
  247.0 1.9 multiply_add_fusion
  248.9 11.3 %shard_map.296 = (f32[400,5120]{1,0:T(8,128)}, f32[47,5120]{1,0:T(8,128)}) custom-call(s32[1]{0:T(128)S(6)} %copy.35.count_ref, bf16[400,5120]{1,0:T(8,128)(2,1)} %bitcast.27, bf16[4,112,5120]{2,1,0:T(8,128)(2,1)} %get-tuple-element.27.part_ref, bf16[4,128,128]{2,1,0:T(8,128)(2,1)} %get-tuple-element.28.corr_ref, f32[48,5120]{1,0:T(8,128)} %get-tuple-element.29.score_ref), custom_call_target="tpu_custom_call" | custom-call | tf_op jit(solution)/shard_map/pallas_call | solution.py:1063
  260.2 0.0 copy-done
  260.2 0.7 copy.36
Async XLA Ops:
  241.4 18.8 %copy-start = (f32[16,2048]{1,0:T(8,128)S(1)}, f32[16,2048]{1,0:T(8,128)}, u32[]{:S(2)}) copy-start(f32[16,2048]{1,0:T(8,128)} %get-tuple-element.33) | copy-start | bytes 393220

commit v2 on v1

--- a/solution.py
+++ b/solution.py
@@ -210,7 +210,9 @@
 WIDE = jnp.float32
 FP = 128
 TILE = 256
-CHUNK = 32
+CHUNK = 16
+LAG = 8
+GROUP = 4
 MESH = pl.DeviceIdType.MESH
 
 
@@ -275,7 +277,6 @@
     gram_sib,
     gram_in,
     gram_all,
-    wbt,
     wht,
     whn,
     small_t,
@@ -296,7 +297,6 @@
     gm_in,
     rows_own,
     rows_all,
-    part_s,
     score_s,
     load_sem,
     soft_sem,
@@ -357,29 +357,17 @@
     for k in range(K):
         wb_own[k, :, 0:F] = wb_ref[:, k * F : (k + 1) * F].astype(LOW)
     wm_own[...] = wm_ref[...].astype(LOW)
-    pl.semaphore_wait(barrier, nch)
-
-    def wb_slot(c):
-        return wb_all.at[:, c, core]
-
-    def wb_send(s):
-        return to_peer(0, s, wb_own, wb_slot(chip))
-
-    def wm_send(s):
-        return to_peer(1, s, wm_own, wm_all.at[chip, core])
-
-    for s in range(1, nch):
-        wb_send(s).start()
-    wb_all[:, chip, core] = wb_own[...]
-    wm_all[chip, core] = wm_own[...]
-
     small_t[...] = jnp.concatenate(
         [small_ref[...], jnp.zeros((FP - small_ref.shape[0], FP), WIDE)], axis=0
     ).T
-
-    load.wait()
-    for s in range(1, nch):
-        wm_send(s).start()
+    wht[...] = jnp.zeros(wht.shape, LOW)
+    wht[0:C, :] = wh_ref[...].astype(LOW)
+    whn[...] = jnp.concatenate(
+        [wh_ref[...], jnp.zeros((FP - C, hid), WIDE)], axis=0
+    ).T.astype(LOW)
+    acc[...] = jnp.zeros(acc.shape, WIDE)
+    wb_all[:, chip, core] = wb_own[...]
+    wm_all[chip, core] = wm_own[...]
 
     width = 2 * TILE
     row_id = lax.broadcasted_iota(jnp.int32, (112, width), 0)
@@ -395,6 +383,7 @@
             xa[k, 112:FP, pl.ds(start, width)] = jnp.zeros((FP - 112, width), LOW)
         return carry
 
+    load.wait()
     cat[K * F : K * F + 16, :] = jnp.zeros((16, nodes), LOW)
     lax.fori_loop(0, nodes // width, build, 0)
 
@@ -402,6 +391,20 @@
     for k in range(K):
         g = dot_nt(xa[k], xa[k])
         gram[pl.ds(k * nch // K, nch // K)] = g.reshape(nch // K, 2, rows_g, FP)
+
+    def wb_send(s):
+        return to_peer(0, s, wb_own, wb_all.at[:, chip, core])
+
+    def wb_pass():
+        return to_sibling(0, wb_all.at[:, :, core], wb_all.at[:, :, core])
+
+    def wm_send(s):
+        return to_peer(1, s, wm_own, wm_all.at[chip, core])
+
+    def wm_pass():
+        return to_sibling(1, wm_all.at[:, core], wm_all.at[:, core])
+
+    pl.semaphore_wait(barrier, nch)
 
     def reduce_one(i, own, sib):
         to_sibling(i, own.at[:, 1 - core], sib).start()
@@ -440,20 +443,16 @@
     reduce_one(2, gram, gram_sib)
     reduce_two(2, gram, gram_sib, gram_in)
     for s in range(1, nch):
-        wb_send(s).wait()
-    to_sibling(0, wb_all.at[:, :, core], wb_all.at[:, :, core]).start()
+        wb_send(s).start()
     reduce_wait(2, gram, gram_in)
     gram_all[chip, core] = total_of(gram_in)
     spread_one(3, gram_all)
-    wht[...] = jnp.zeros(wht.shape, LOW)
-    wht[0:C, :] = wh_ref[...].astype(LOW)
-    whn[...] = jnp.concatenate(
-        [wh_ref[...], jnp.zeros((FP - C, hid), WIDE)], axis=0
-    ).T.astype(LOW)
-    acc[...] = jnp.zeros(acc.shape, WIDE)
-    to_sibling(0, wb_all.at[:, :, core], wb_all.at[:, :, core]).wait()
-    for k in range(K):
-        wbt[k] = wb_all[k].reshape(hid, FP).astype(WIDE).T.astype(LOW)
+    for s in range(1, nch):
+        wb_send(s).wait()
+    wb_pass().start()
+    for s in range(1, nch):
+        wm_send(s).start()
+    wb_pass().wait()
     spread_two(3, gram_all)
     spread_wait(3, gram_all)
 
@@ -499,72 +498,73 @@
             cols[1, there, :] = jnp.broadcast_to(1.0 - slope2, (FP, FP))
             cols[2, there, :] = jnp.broadcast_to(ginv, (FP, FP))
 
-    for s in range(1, nch):
-        wm_send(s).wait()
-    to_sibling(1, wm_all.at[:, core], wm_all.at[:, core]).start()
-    to_sibling(1, wm_all.at[:, core], wm_all.at[:, core]).wait()
-
     def branch_dot(k, j):
         x = xa[k, :, pl.ds(pl.multiple_of(j * TILE, TILE), TILE)]
         pre_s[k % 2] = dot_nn(wp[k], jnp.concatenate([x, x], axis=0))
 
-    def mid_dot(k, slot, start):
-        w = wm_all[:, :, :, k * hid : (k + 1) * hid].reshape(hid, hid)
-        d = dot_nn(w, cat_s[slot, k * hid : (k + 1) * hid, :])
-        if k == 0:
-            mid_z[:, pl.ds(start, TILE)] = d
-            return
-        z = mid_z[:, pl.ds(start, TILE)] + d
-        mid_z[:, pl.ds(start, TILE)] = z
-        if k == K - 1:
-            masked = z * mask_row(start, TILE)
-            acc[0] += fold_halves(masked)
-            acc[1] += fold_halves(masked * z)
-
-    def forward_chunk(k, r, slot, start):
-        rows = slice(k * hid + r, k * hid + r + CHUNK)
+    def mid_dot(j):
+        at = pl.ds(pl.multiple_of(j * TILE, TILE), TILE)
+        mid_z[:, at] = dot_nn(wm_all[...].reshape(hid, K * hid), cat[:, at])
+        here = mask_row(j * TILE, TILE)
+        for r in range(0, hid, CHUNK):
+            rows = slice(r, r + CHUNK)
+            z = mid_z[rows, at]
+            masked = z * here
+            acc[0, rows, :] += fold_halves(masked)
+            acc[1, rows, :] += fold_halves(masked * z)
+
+    def forward_chunk(k, j, r, slot):
+        rows = slice(r, r + CHUNK)
+        wide_rows = slice(k * hid + r, k * hid + r + CHUNK)
         for half in range(2):
             lanes = slice(half * 128, half * 128 + 128)
-            u1 = pre_s[k % 2, r : r + CHUNK, lanes]
+            u1 = pre_s[k % 2, rows, lanes]
             m1 = soft_two(u1)
-            u2 = u1 - cols[0, rows, :] * m1
+            u2 = u1 - cols[0, wide_rows, :] * m1
             m2 = soft_two(u2)
-            v = ((u2 - cols[1, rows, :] * m2) * -LN2).astype(LOW)
-            cat_s[slot, rows, lanes] = v
-            cat[rows, pl.ds(start + half * 128, 128)] = v
-            soft_s[slot, 0, rows, lanes] = m1.astype(LOW)
-            soft_s[slot, 1, rows, lanes] = m2.astype(LOW)
+            v = ((u2 - cols[1, wide_rows, :] * m2) * -LN2).astype(LOW)
+            cat[wide_rows, pl.ds(pl.multiple_of(j * TILE + half * 128, 128), 128)] = v
+            soft_s[slot, 0, k, rows, lanes] = m1.astype(LOW)
+            soft_s[slot, 1, k, rows, lanes] = m2.astype(LOW)
 
     def soft_save(slot, j):
-        return pltpu.make_async_copy(soft_s.at[slot], soft_hbm.at[j], soft_sem.at[slot])
-
-    cat_s[1] = jnp.zeros(cat_s.shape[1:], LOW)
+        return pltpu.make_async_copy(soft_s.at[slot], soft_hbm.at[:, j], soft_sem.at[slot])
+
+    def forward(mids):
+        def body(i, carry):
+            for slot in range(2):
+                j = i * 2 + slot
+                soft_save(slot, j).wait()
+                if mids:
+                    mid_dot(j - LAG)
+                for k in range(K):
+                    if k < K - 1:
+                        branch_dot(k + 1, j)
+                    else:
+                        branch_dot(0, jnp.minimum(j + 1, tiles - 1))
+                    for r in range(0, hid, CHUNK):
+                        forward_chunk(k, j, r, slot)
+                soft_save(slot, j).start()
+            return carry
+
+        return body
+
+    for slot in range(2):
+        soft_save(slot, slot).start()
     branch_dot(0, 0)
-
-    def forward(i, carry):
-        for slot in range(2):
-            j = i * 2 + slot
-
-            @pl.when(i > 0)
-            def _():
-                soft_save(slot, j - 2).wait()
-
-            start = pl.multiple_of(j * TILE, TILE)
-            before = pl.multiple_of(jnp.maximum(j - 1, 0) * TILE, TILE)
-            for k in range(K):
-                mid_dot(k, 1 - slot, before)
-                if k < K - 1:
-                    branch_dot(k + 1, j)
-                else:
-                    branch_dot(0, jnp.minimum(j + 1, tiles - 1))
-                for r in range(0, hid, CHUNK):
-                    forward_chunk(k, r, slot, start)
-            soft_save(slot, j).start()
+    lax.fori_loop(0, LAG // 2, forward(False), 0)
+    for s in range(1, nch):
+        wm_send(s).wait()
+    wm_pass().start()
+    wm_pass().wait()
+    lax.fori_loop(LAG // 2, tiles // 2, forward(True), 0)
+
+    def mid_rest(i, carry):
+        mid_dot(2 * i)
+        mid_dot(2 * i + 1)
         return carry
 
-    lax.fori_loop(0, tiles // 2, forward, 0)
-    for k in range(K):
-        mid_dot(k, 1, (tiles - 1) * TILE)
+    lax.fori_loop((tiles - LAG) // 2, tiles // 2, mid_rest, 0)
     for slot in range(2):
         soft_save(slot, tiles - 2 + slot).wait()
 
@@ -599,6 +599,10 @@
         ginv = cols[2, rows, :]
         cols[0, rows, :] = ginv * (1.0 - c1)
         cols[2, rows, :] = ginv * c1
+    for k in range(K):
+        w = wb_all[k].reshape(hid, FP).astype(WIDE).T.astype(LOW)
+        wp[2, k * FP : (k + 1) * FP, :] = w[:, 0:TILE]
+        wp[3, k * FP : (k + 1) * FP, :] = w[:, TILE : 2 * TILE]
     for q in range(4):
         w = wm_all[q * nch // 4 : (q + 1) * nch // 4].reshape(FP, 2048)
         w = w.T
@@ -653,9 +657,9 @@
                     u = z * bn2[0, rows, :] + bn2[1, rows, :]
                     m = soft_two(u)
                     v = (u - bn2[3, rows, :] * m) * -LN2
-                    soft_s[0, 0, rows, lanes] = v.astype(LOW)
+                    soft_s[0, 0, 0, rows, lanes] = v.astype(LOW)
                     pre_s[0, rows, lanes] = m
-            s = dot_nn(wht[...], soft_s[0, 0, 0:hid, :]) + bias_col
+            s = dot_nn(wht[...], soft_s[0, 0, 0]) + bias_col
             score_s[slot] = s * here
             s = jnp.where(class_id < C, s, -1e30)
             e = jnp.exp(s - jnp.max(s, axis=0, keepdims=True))
@@ -665,7 +669,7 @@
             hot = (class_id == code).astype(WIDE)
             g = ((p - hot) * trained).astype(LOW)
             bias_acc[...] += fold_halves(g.astype(WIDE))
-            head_acc[...] += dot_nt(g, soft_s[0, 0, 0:hid, :])
+            head_acc[...] += dot_nt(g, soft_s[0, 0, 0])
             pre_s[1] = dot_nn(whn[:, 0:48], g)
             for r in range(0, hid, CHUNK):
                 rows = slice(r, r + CHUNK)
@@ -746,99 +750,114 @@
     to_sibling(6, head_loc.at[:, 1 - core], head_sib).wait()
     reduce_two(6, head_loc, head_sib, head_in)
 
+    width_m = K * hid
+
     def mid_grad(i, carry):
-        at = pl.multiple_of(i * TILE, TILE)
-        mid_z[:, pl.ds(at, TILE)] = dot_nt(dz[...], cat[pl.ds(at, TILE), :])
+        at = pl.ds(pl.multiple_of(i * TILE, TILE), TILE)
+        pre_s[0] = dot_nt(dz[...], cat[at, :])
+        for c in range(nch):
+            first = pre_s[0, 2 * c * rb : (2 * c + 1) * rb, :]
+            second = pre_s[0, (2 * c + 1) * rb : (2 * c + 2) * rb, :]
+            mid_z[c * rb : (c + 1) * rb, at] = jnp.where(core == 0, first, second)
+            wm_all[c, 0, :, at] = jnp.where(core == 0, second, first).astype(LOW)
         return carry
 
-    lax.fori_loop(0, K * hid // TILE, mid_grad, 0)
-    width_m = K * hid
-
-    for c in range(nch):
-        for e in range(2):
-            at = (2 * c + e) * rb
-
-            @pl.when(core != e)
-            def _():
-                wm_all[c, 0] = mid_z[at : at + rb, 0:width_m].astype(LOW)
-
+    lax.fori_loop(0, width_m // TILE, mid_grad, 0)
     to_sibling(8, wm_all.at[:, 0], wm_all.at[:, 1]).start()
     reduce_wait(6, head_loc, head_in)
     head_all[chip, core] = total_of(head_in)
     spread_one(7, head_all)
 
-    def soft_load(slot, k, j):
+    groups = tiles // GROUP
+
+    def soft_load(t):
+        k = lax.div(t, groups)
+        g = lax.rem(t, groups)
+        slot = lax.rem(t, 2)
         return pltpu.make_async_copy(
-            soft_hbm.at[j, :, pl.ds(k * hid, hid), :],
-            soft_s.at[slot, :, pl.ds(0, hid), :],
-            soft_sem.at[slot],
+            soft_hbm.at[:, pl.ds(g * GROUP, GROUP), k], soft_s.at[slot], soft_sem.at[slot]
         )
 
-    def part_save(slot, k, j):
+    def part_save(k):
         return pltpu.make_async_copy(
-            part_s.at[slot],
-            part_hbm.at[k, :, pl.ds(pl.multiple_of(j * TILE, TILE), TILE)],
-            part_sem.at[slot],
+            cat.at[pl.ds(k * 112, 112), :], part_hbm.at[k], part_sem.at[k]
         )
 
-    def back_dot(k, j, slot):
-        w = jnp.concatenate(
-            [cat_s[0, k * hid : (k + 1) * hid, :], cat_s[1, k * hid : (k + 1) * hid, :]], axis=1
-        )
-        pre_s[slot] = dot_nn(w, dz[:, pl.ds(pl.multiple_of(j * TILE, TILE), TILE)])
-
-    def tail_dots(k, j, slot):
-        t = soft_s[slot, 0, hid : 2 * hid, :]
+    def back_dot(k, j, slot, half):
+        rows = slice(half * hid // 2, (half + 1) * hid // 2)
+        at = slice(k * hid + half * hid // 2, k * hid + (half + 1) * hid // 2)
+        w = jnp.concatenate([cat_s[0, at, :], cat_s[1, at, :]], axis=1)
+        pre_s[slot, rows, :] = dot_nn(w, dz[:, pl.ds(pl.multiple_of(j * TILE, TILE), TILE)])
+
+    def turned(k):
+        rows = slice(k * FP, (k + 1) * FP)
+        return jnp.concatenate([wp[2, rows, :], wp[3, rows, :]], axis=1)
+
+    def sum_dot(k, j, slot):
         x = xa[k, :, pl.ds(pl.multiple_of(j * TILE, TILE), TILE)]
-        acc[2] += dot_nt(t, x)
-        part_s[slot] = dot_nn(wbt[k, 0 : part_s.shape[1], :], t).astype(LOW)
-
+        acc[2] += dot_nt(wp[slot], x)
+
+    def part_dot(k, j, slot):
+        at = pl.ds(pl.multiple_of(j * TILE, TILE), TILE)
+        cat[k * 112 : (k + 1) * 112, at] = dot_nn(turned(k)[0:112], wp[slot]).astype(LOW)
+
+    for t in range(2):
+        soft_load(t).start()
     for k in range(K):
         acc[0] = jnp.zeros(acc.shape[1:], WIDE)
         acc[1] = jnp.zeros(acc.shape[1:], WIDE)
         acc[2] = jnp.zeros(acc.shape[1:], WIDE)
-        for slot in range(2):
-            soft_load(slot, k, slot).start()
-        back_dot(k, 0, 0)
-
-        def backward(i, carry):
-            for slot in range(2):
-                j = i * 2 + slot
-                soft_load(slot, k, j).wait()
-
-                @pl.when(i > 0)
-                def _():
-                    part_save(slot, k, j - 2).wait()
-
-                back_dot(k, jnp.minimum(j + 1, tiles - 1), 1 - slot)
-                for r in range(0, hid, CHUNK):
-                    rows = slice(r, r + CHUNK)
-                    wide_rows = slice(k * hid + r, k * hid + r + CHUNK)
-                    sums = [0.0, 0.0]
-                    for half in range(2):
-                        lanes = slice(half * 128, half * 128 + 128)
-                        d = pre_s[slot, rows, lanes]
-                        m1 = soft_s[slot, 0, rows, lanes].astype(WIDE)
-                        m2 = soft_s[slot, 1, rows, lanes].astype(WIDE)
-                        c2 = cols[1, wide_rows, :]
-                        da = d * ((1.0 - c2) + c2 * jnp.exp2(-m2))
-                        t = da * (cols[0, wide_rows, :] + cols[2, wide_rows, :] * jnp.exp2(-m1))
-                        sums[0] += d * m2
-                        sums[1] += da * m1
-                        soft_s[slot, 0, hid + r : hid + r + CHUNK, lanes] = t.astype(LOW)
-                    acc[0, rows, :] += sums[0]
-                    acc[1, rows, :] += sums[1]
-                tail_dots(k, j, slot)
-                part_save(slot, k, j).start()
-
-                @pl.when(i < tiles // 2 - 1)
-                def _():
-                    soft_load(slot, k, j + 2).start()
+        wp[1] = jnp.zeros(wp.shape[1:], LOW)
+        back_dot(k, 0, 0, 0)
+        back_dot(k, 0, 0, 1)
+
+        def backward(g, carry):
+            t = k * groups + g
+            side = lax.rem(t, 2)
+            soft_load(t).wait()
+            for q in range(GROUP):
+                j = g * GROUP + q
+                slot = q % 2
+                after = jnp.minimum(j + 1, tiles - 1)
+                before = jnp.maximum(j - 1, 0)
+                parts = [
+                    functools.partial(back_dot, k, after, 1 - slot, 0),
+                    functools.partial(back_dot, k, after, 1 - slot, 1),
+                    functools.partial(sum_dot, k, before, 1 - slot),
+                    functools.partial(part_dot, k, before, 1 - slot),
+                ]
+                for n, part in enumerate(parts):
+                    part()
+                    for r in range(n * hid // 4, (n + 1) * hid // 4, CHUNK):
+                        rows = slice(r, r + CHUNK)
+                        wide_rows = slice(k * hid + r, k * hid + r + CHUNK)
+                        sums = [0.0, 0.0]
+                        for half in range(2):
+                            lanes = slice(half * 128, half * 128 + 128)
+                            d = pre_s[slot, rows, lanes]
+                            m1 = soft_s[side, 0, q, rows, lanes].astype(WIDE)
+                            m2 = soft_s[side, 1, q, rows, lanes].astype(WIDE)
+                            c2 = cols[1, wide_rows, :]
+                            da = d * ((1.0 - c2) + c2 * jnp.exp2(-m2))
+                            v = da * (
+                                cols[0, wide_rows, :] + cols[2, wide_rows, :] * jnp.exp2(-m1)
+                            )
+                            sums[0] += d * m2
+                            sums[1] += da * m1
+                            wp[slot, rows, lanes] = v.astype(LOW)
+                        acc[0, rows, :] += sums[0]
+                        acc[1, rows, :] += sums[1]
+
+            @pl.when(t + 2 < K * groups)
+            def _():
+                soft_load(t + 2).start()
+
             return carry
 
-        lax.fori_loop(0, tiles // 2, backward, 0)
-        for slot in range(2):
-            part_save(slot, k, tiles - 2 + slot).wait()
+        lax.fori_loop(0, groups, backward, 0)
+        sum_dot(k, tiles - 1, 1)
+        part_dot(k, tiles - 1, 1)
+        part_save(k).start()
 
         two = lax.broadcasted_iota(jnp.int32, (hid, FP), 1)
         sl2 = jnp.sum(acc[0], axis=1, keepdims=True) * -LN2
@@ -852,14 +871,8 @@
         if k == 0:
             to_sibling(8, wm_all.at[:, 0], wm_all.at[:, 1]).wait()
             for c in range(nch):
-                for e in range(2):
-                    at = (2 * c + e) * rb
-
-                    @pl.when(core == e)
-                    def _():
-                        v = mid_z[at : at + rb, 0:width_m] + wm_all[c, 1].astype(WIDE)
-                        wm_all[c, 0] = v.astype(LOW)
-
+                v = mid_z[c * rb : (c + 1) * rb, 0:width_m] + wm_all[c, 1].astype(WIDE)
+                wm_all[c, 0] = v.astype(LOW)
             for s in range(1, nch):
                 to_peer(8, s, wm_all.at[lax.rem(chip + s, nch), 0], gm_in.at[chip]).start()
             gm_in[chip] = wm_all[chip, 0]
@@ -878,6 +891,9 @@
     gm_out[...] = total_of(gm_in)
     for k in range(K - 2, K):
         reduce_wait(9 + k, pgrad.at[k % 2], pgrad_in.at[k])
+
+    for k in range(K):
+        part_save(k).wait()
 
     lane_s = lax.broadcasted_iota(jnp.int32, (rb, FP), 1)
     quant = []
@@ -934,15 +950,29 @@
     for q in range(blocks):
         head_out[:, q * FP : (q + 1) * FP] = head_flat[q * 48 : q * 48 + 48]
     for k in range(K):
-        wt = wbt[k].astype(WIDE)
+        wt = turned(k).astype(WIDE)
         r0 = jnp.concatenate([full[k * blocks + q][4:5] for q in range(blocks)], axis=1)
         r1 = jnp.concatenate([full[k * blocks + q][5:6] for q in range(blocks)], axis=1)
-        m = dot_nn((wt * r0).astype(LOW), wb_all[k].reshape(hid, FP))
+        m = dot_nt((wt * r0).astype(LOW), turned(k))
         v = jnp.sum(wt * r1, axis=1, keepdims=True)
         corr_out[k] = jnp.where(lane == F, v, m).astype(LOW)
 
 
-def finish_kernel(count_ref, feats_ref, part_ref, corr_ref, score_ref, grad_ref, logit_ref):
+def finish_kernel(
+    root,
+    count_ref,
+    feats_ref,
+    part_ref,
+    corr_ref,
+    score_ref,
+    gm_ref,
+    gb_ref,
+    gh_ref,
+    *refs,
+):
+    states, outs = refs[:9], refs[9:]
+    grad_ref, logit_ref, grad_b, grad_h = outs[:4]
+    new = outs[4:]
     width = feats_ref.shape[1]
     lane = lax.broadcasted_iota(jnp.int32, (1, width), 1) + pl.program_id(0) * width
     here = (lane < count_ref[0]).astype(WIDE)
@@ -956,6 +986,19 @@
         out = part_ref[k].astype(WIDE) - fix
         grad_ref[k * F : (k + 1) * F, :] = out[0:F]
     logit_ref[...] = score_ref[0:C, :]
+
+    @pl.when(pl.program_id(0) == 0)
+    def _():
+        g = jnp.concatenate([gb_ref[k][:, 0:F] for k in range(K)], axis=1)
+        grad_b[...] = g
+        grad_h[...] = gh_ref[0:C, :]
+        for n, (grad, rate) in enumerate(
+            ((g, 0.8 / root), (gm_ref[...], 0.08 / root), (gh_ref[0:C, :], 0.3 / root))
+        ):
+            w, m, a = (r[...] for r in states[3 * n : 3 * n + 3])
+            res = nesterov(w, grad, m, a, rate)
+            for r, v in zip(new[3 * n : 3 * n + 3], res):
+                r[...] = v
 
 
 def fused(
@@ -998,7 +1041,7 @@
         out_shape=(
             jax.ShapeDtypeStruct((48, nodes), WIDE),
             jax.ShapeDtypeStruct((K, 112, nodes), LOW),
-            jax.ShapeDtypeStruct((tiles, 2, width_m, TILE), LOW),
+            jax.ShapeDtypeStruct((2, tiles, K, H, TILE), LOW),
             jax.ShapeDtypeStruct((rb, width_m), WIDE),
             jax.ShapeDtypeStruct((K, rb, FP), WIDE),
             jax.ShapeDtypeStruct((48, H), WIDE),
@@ -1013,7 +1056,7 @@
             pltpu.VMEM((H, nodes), WIDE),
             pltpu.VMEM((H, nodes), LOW),
             pltpu.VMEM((2, width_m, TILE), LOW),
-            pltpu.VMEM((2, 2, width_m, TILE), LOW),
+            pltpu.VMEM((2, 2, K, H, TILE), LOW),
             pltpu.VMEM((2, H, TILE), WIDE),
             pltpu.VMEM((K, H, 2 * FP), LOW),
             pltpu.VMEM((3, width_m, FP), WIDE),
@@ -1025,7 +1068,6 @@
             pltpu.VMEM((nch, rows_g, FP), WIDE),
             pltpu.VMEM((nch, rows_g, FP), WIDE),
             pltpu.VMEM((nch, 2, rows_g, FP), WIDE),
-            pltpu.VMEM((K, FP, H), LOW),
             pltpu.VMEM((48, H), LOW),
             pltpu.VMEM((H, FP), LOW),
             pltpu.VMEM((FP, FP), WIDE),
@@ -1046,11 +1088,10 @@
             pltpu.VMEM((nch, rb, width_m), LOW),
             pltpu.VMEM((8, FP), WIDE),
             pltpu.VMEM((nch, 2, 8, FP), WIDE),
-            pltpu.VMEM((2, 112, TILE), LOW),
             pltpu.VMEM((2, 48, TILE), WIDE),
             pltpu.SemaphoreType.DMA((1,)),
             pltpu.SemaphoreType.DMA((2,)),
-            pltpu.SemaphoreType.DMA((2,)),
+            pltpu.SemaphoreType.DMA((K,)),
             pltpu.SemaphoreType.DMA((2,)),
             pltpu.SemaphoreType.DMA((14, nch)),
             pltpu.SemaphoreType.DMA((14, nch)),
@@ -1059,41 +1100,56 @@
             collective_id=0, has_side_effects=True, vmem_limit_bytes=65400 * 1024
         ),
     )(counts, feats, code, w_branch.T, w_mid.T, w_head.T, small)
-    step = 512
-    fgrad, logits = pl.pallas_call(
-        finish_kernel,
+    step = nodes // 2
+    root = math.sqrt(nodes * devices)
+
+    def whole(v):
+        return pl.BlockSpec(v.shape, lambda i: (0,) * len(v.shape))
+
+    states = (
+        w_branch.T,
+        mom_branch.T,
+        avg_branch.T,
+        w_mid.T,
+        mom_mid.T,
+        avg_mid.T,
+        w_head.T,
+        mom_head.T,
+        avg_head.T,
+    )
+    shapes = [jax.ShapeDtypeStruct(v.shape, WIDE) for v in (states[0], states[6]) + states]
+    fgrad, logits, grad_b, grad_h, *new = pl.pallas_call(
+        functools.partial(finish_kernel, root),
         grid=(nodes // step,),
-        out_shape=(
+        out_shape=[
             jax.ShapeDtypeStruct((K * F, nodes), WIDE),
             jax.ShapeDtypeStruct((C, nodes), WIDE),
-        ),
+        ]
+        + shapes,
         in_specs=[
             smem,
             pl.BlockSpec((K * F, step), lambda i: (0, i)),
             pl.BlockSpec((K, 112, step), lambda i: (0, 0, i)),
             pl.BlockSpec((K, FP, FP), lambda i: (0, 0, 0)),
             pl.BlockSpec((48, step), lambda i: (0, i)),
-        ],
-        out_specs=(
+        ]
+        + [whole(v) for v in (gm, gb, gh) + states],
+        out_specs=[
             pl.BlockSpec((K * F, step), lambda i: (0, i)),
             pl.BlockSpec((C, step), lambda i: (0, i)),
-        ),
-    )(counts, feats, part, corr, scores)
-    root = math.sqrt(nodes * devices)
-    grad_branch = jnp.concatenate([gb[k, :, :F] for k in range(K)], axis=1).T
-    grad_mid = gm.T
-    grad_head = gh[:C].T
+        ]
+        + [whole(v) for v in shapes],
+        compiler_params=pltpu.CompilerParams(vmem_limit_bytes=65400 * 1024),
+    )(counts, feats, part, corr, scores, gm, gb, gh, *states)
     grad_small = gs.reshape(-1)[: small_params.shape[0]]
-    mom_b, avg_b, new_b = nesterov(w_branch, grad_branch, mom_branch, avg_branch, 0.8 / root)
-    mom_m, avg_m, new_m = nesterov(w_mid, grad_mid, mom_mid, avg_mid, 0.08 / root)
-    mom_h, avg_h, new_h = nesterov(w_head, grad_head, mom_head, avg_head, 0.3 / root)
+    mom_b, avg_b, new_b, mom_m, avg_m, new_m, mom_h, avg_h, new_h = (v.T for v in new)
     mom_s, avg_s, new_s = nesterov(small_params, grad_small, mom_small, avg_small, 1.0 / root)
     return (
         logits.T,
         fgrad.T,
-        grad_branch,
-        grad_mid,
-        grad_head,
+        grad_b.T,
+        gm.T,
+        grad_h.T,
         grad_small,
         mom_b,
         mom_m,

time: 263 us -> 215 us (0.82)
  Pallas kernels: 249 us -> 207 us
  other arithmetic: 8.04 us -> 2.86 us
    pallas_call x1, Pallas kernels: 237 us -> 199 us  [fused(): pl.pallas_call(functools.partial(net_kernel, nch), out_shape=(jax.ShapeDt...]
    add x4 -> x1, other arithmetic: 6.69 us -> 1.51 us  [nesterov(): average_new = DECAY * average_old + (1.0 - DECAY) * weight_new]
    pallas_call x1, Pallas kernels: 11.3 us -> 8.46 us  [fused(): pl.pallas_call(functools.partial(finish_kernel, root), grid=(nodes // ste...]
where the time goes in v2:
time: 215 us
  Pallas kernels  207 us (96%)
  local copies, waits for them, and re-layouts  2.97 us (1%)
  other arithmetic  2.86 us (1%)
    pallas_call x1, Pallas kernels, fused(): pl.pallas_call(functools.partial(net_kernel, nch), out_shape=(jax.ShapeDt...  199 us
    pallas_call x1, Pallas kernels, fused(): pl.pallas_call(functools.partial(finish_kernel, root), grid=(nodes // ste...  8.46 us

profile of v2, /device:TPU:0, one launch (start us, length us, event | category | flops | bytes accessed | tf_op | source)
XLA Modules:
  0.0 214.6 jit_solution(7359196759851775872)
XLA Ops:
  1.3 1.4 compare_select_fusion
  2.7 1.4 pad_bitcast_fusion.small_ref
  4.1 199.0 %shard_map.295 = (f32[48,5120]{1,0:T(8,128)}, bf16[4,112,5120]{2,1,0:T(8,128)(2,1)}, bf16[2,20,4,512,256]{4,3,2,1,0:T(8,128)(2,1)}, f32[16,2048]{1,0:T(8,128)}, ...) custom-call(s32[1]{0:T(128)S(6)} %copy.35.count_ref, ...), custom_call_target="tpu_custom_call" | custom-call | tf_op jit(solution)/shard_map/pallas_call | solution.py:1039
  203.0 1.5 multiply_add_fusion
  204.6 8.5 %shard_map.296 = (f32[400,5120]{1,0:T(8,128)}, f32[47,5120]{1,0:T(8,128)}, f32[16,400]{1,0:T(8,128)}, f32[47,512]{1,0:T(8,128)}, f32[16,400]{1,0:T(8,128)}, /*in...) custom-call(s32[1]{0:T(128)S(6)} %copy.35.count_ref, ...), custom_call_target="tpu_custom_call" | custom-call | tf_op jit(solution)/shard_map/pallas_call | solution.py:1121
  213.0 1.6 copy.36

commit v3 on v2

--- a/solution.py
+++ b/solution.py
@@ -211,7 +211,7 @@
 FP = 128
 TILE = 256
 CHUNK = 16
-LAG = 8
+LAG = 10
 GROUP = 4
 MESH = pl.DeviceIdType.MESH
 
@@ -247,7 +247,8 @@
     nch,
     count_ref,
     feats_hbm,
-    code_ref,
+    label_ref,
+    marked_ref,
     wb_ref,
     wm_ref,
     wh_ref,
@@ -353,22 +354,6 @@
         pl.semaphore_signal(barrier, inc=1, device_id=(peer(s),), device_id_type=MESH)
     pl.semaphore_signal(barrier, inc=1, device_id=(sibling,), device_id_type=MESH)
 
-    wb_own[...] = jnp.zeros(wb_own.shape, LOW)
-    for k in range(K):
-        wb_own[k, :, 0:F] = wb_ref[:, k * F : (k + 1) * F].astype(LOW)
-    wm_own[...] = wm_ref[...].astype(LOW)
-    small_t[...] = jnp.concatenate(
-        [small_ref[...], jnp.zeros((FP - small_ref.shape[0], FP), WIDE)], axis=0
-    ).T
-    wht[...] = jnp.zeros(wht.shape, LOW)
-    wht[0:C, :] = wh_ref[...].astype(LOW)
-    whn[...] = jnp.concatenate(
-        [wh_ref[...], jnp.zeros((FP - C, hid), WIDE)], axis=0
-    ).T.astype(LOW)
-    acc[...] = jnp.zeros(acc.shape, WIDE)
-    wb_all[:, chip, core] = wb_own[...]
-    wm_all[chip, core] = wm_own[...]
-
     width = 2 * TILE
     row_id = lax.broadcasted_iota(jnp.int32, (112, width), 0)
 
@@ -406,10 +391,6 @@
 
     pl.semaphore_wait(barrier, nch)
 
-    def reduce_one(i, own, sib):
-        to_sibling(i, own.at[:, 1 - core], sib).start()
-        to_sibling(i, own.at[:, 1 - core], sib).wait()
-
     def reduce_two(i, own, sib, got):
         own[:, core] = own[:, core] + sib[...]
         for s in range(1, nch):
@@ -440,10 +421,27 @@
     def spread_wait(i, every):
         to_sibling(i, every.at[:, core], every.at[:, core]).wait()
 
-    reduce_one(2, gram, gram_sib)
+    to_sibling(2, gram.at[:, 1 - core], gram_sib).start()
+    wb_own[...] = jnp.zeros(wb_own.shape, LOW)
+    for k in range(K):
+        wb_own[k, :, 0:F] = wb_ref[:, k * F : (k + 1) * F].astype(LOW)
+    wb_all[:, chip, core] = wb_own[...]
+    to_sibling(2, gram.at[:, 1 - core], gram_sib).wait()
     reduce_two(2, gram, gram_sib, gram_in)
     for s in range(1, nch):
         wb_send(s).start()
+    small_t[...] = jnp.concatenate(
+        [small_ref[...], jnp.zeros((FP - small_ref.shape[0], FP), WIDE)], axis=0
+    ).T
+    wht[...] = jnp.zeros(wht.shape, LOW)
+    wht[0:C, :] = wh_ref[...].astype(LOW)
+    whn[...] = jnp.concatenate(
+        [wh_ref[...], jnp.zeros((FP - C, hid), WIDE)], axis=0
+    ).T.astype(LOW)
+    acc[...] = jnp.zeros(acc.shape, WIDE)
+    wm_own[...] = wm_ref[...].astype(LOW)
+    wm_all[chip, core] = wm_own[...]
+
     reduce_wait(2, gram, gram_in)
     gram_all[chip, core] = total_of(gram_in)
     spread_one(3, gram_all)
@@ -640,13 +638,13 @@
         )
 
     def head(i, carry):
+        @pl.when(i > 0)
+        def _():
+            for slot in range(2):
+                score_save(slot, 2 * i - 2 + slot).wait()
+
         for slot in range(2):
             j = i * 2 + slot
-
-            @pl.when(i > 0)
-            def _():
-                score_save(slot, j - 2).wait()
-
             start = pl.multiple_of(j * TILE, TILE)
             here = mask_row(start, TILE)
             for r in range(0, hid, CHUNK):
@@ -657,27 +655,26 @@
                     u = z * bn2[0, rows, :] + bn2[1, rows, :]
                     m = soft_two(u)
                     v = (u - bn2[3, rows, :] * m) * -LN2
-                    soft_s[0, 0, 0, rows, lanes] = v.astype(LOW)
-                    pre_s[0, rows, lanes] = m
-            s = dot_nn(wht[...], soft_s[0, 0, 0]) + bias_col
+                    soft_s[slot, 0, 0, rows, lanes] = v.astype(LOW)
+                    soft_s[slot, 1, 0, rows, lanes] = m.astype(LOW)
+            s = dot_nn(wht[...], soft_s[slot, 0, 0]) + bias_col
             score_s[slot] = s * here
             s = jnp.where(class_id < C, s, -1e30)
             e = jnp.exp(s - jnp.max(s, axis=0, keepdims=True))
             p = e / jnp.sum(e, axis=0, keepdims=True)
-            code = code_ref[:, pl.ds(start, TILE)]
-            trained = here * (code >= 0).astype(WIDE)
-            hot = (class_id == code).astype(WIDE)
+            trained = here * marked_ref[:, pl.ds(start, TILE)].astype(WIDE)
+            hot = (class_id == label_ref[:, pl.ds(start, TILE)]).astype(WIDE)
             g = ((p - hot) * trained).astype(LOW)
             bias_acc[...] += fold_halves(g.astype(WIDE))
-            head_acc[...] += dot_nt(g, soft_s[0, 0, 0])
-            pre_s[1] = dot_nn(whn[:, 0:48], g)
+            head_acc[...] += dot_nt(g, soft_s[slot, 0, 0])
+            pre_s[slot] = dot_nn(whn[:, 0:48], g)
             for r in range(0, hid, CHUNK):
                 rows = slice(r, r + CHUNK)
                 sums = [0.0, 0.0, 0.0]
                 for half in range(2):
                     lanes = slice(half * 128, half * 128 + 128)
-                    d = pre_s[1, rows, lanes]
-                    m = pre_s[0, rows, lanes]
+                    d = pre_s[slot, rows, lanes]
+                    m = soft_s[slot, 1, 0, rows, lanes].astype(WIDE)
                     c3 = bn2[3, rows, :]
                     dy = d * ((1.0 - c3) + c3 * jnp.exp2(-m))
                     z = mid_z[rows, pl.ds(start + half * 128, 128)] - bn2[2, rows, :]
@@ -687,7 +684,8 @@
                     dz[rows, pl.ds(start + half * 128, 128)] = dy.astype(LOW)
                 for q in range(3):
                     acc[q, rows, :] += sums[q]
-            score_save(slot, j).start()
+        for slot in range(2):
+            score_save(slot, 2 * i + slot).start()
         return carry
 
     lax.fori_loop(0, tiles // 2, head, 0)
@@ -762,8 +760,40 @@
             wm_all[c, 0, :, at] = jnp.where(core == 0, second, first).astype(LOW)
         return carry
 
-    lax.fori_loop(0, width_m // TILE, mid_grad, 0)
-    to_sibling(8, wm_all.at[:, 0], wm_all.at[:, 1]).start()
+    piece = width_m // K
+
+    def mid_slot(c):
+        return 8 if c == 0 else 13 + c
+
+    def mid_pass(c):
+        at = pl.ds(c * piece, piece)
+        return to_sibling(mid_slot(c), wm_all.at[:, 0, :, at], wm_all.at[:, 1, :, at])
+
+    def mid_send(c, s):
+        at = pl.ds(c * piece, piece)
+        return to_peer(
+            mid_slot(c),
+            s,
+            wm_all.at[lax.rem(chip + s, nch), 0, :, at],
+            gm_in.at[chip, :, at],
+        )
+
+    def mid_add(c):
+        mid_pass(c).wait()
+        at = slice(c * piece, (c + 1) * piece)
+        for n in range(nch):
+            v = mid_z[n * rb : (n + 1) * rb, at] + wm_all[n, 1, :, at].astype(WIDE)
+            wm_all[n, 0, :, at] = v.astype(LOW)
+        for s in range(1, nch):
+            mid_send(c, s).start()
+        gm_in[chip, :, at] = wm_all[chip, 0, :, at]
+
+    steps = piece // TILE
+    for c in range(K):
+        lax.fori_loop(c * steps, (c + 1) * steps, mid_grad, 0)
+        mid_pass(c).start()
+        if c > 0:
+            mid_add(c - 1)
     reduce_wait(6, head_loc, head_in)
     head_all[chip, core] = total_of(head_in)
     spread_one(7, head_all)
@@ -780,7 +810,7 @@
 
     def part_save(k):
         return pltpu.make_async_copy(
-            cat.at[pl.ds(k * 112, 112), :], part_hbm.at[k], part_sem.at[k]
+            dz.at[pl.ds(k * 112, 112), :], part_hbm.at[k], part_sem.at[k]
         )
 
     def back_dot(k, j, slot, half):
@@ -797,9 +827,16 @@
         x = xa[k, :, pl.ds(pl.multiple_of(j * TILE, TILE), TILE)]
         acc[2] += dot_nt(wp[slot], x)
 
-    def part_dot(k, j, slot):
-        at = pl.ds(pl.multiple_of(j * TILE, TILE), TILE)
-        cat[k * 112 : (k + 1) * 112, at] = dot_nn(turned(k)[0:112], wp[slot]).astype(LOW)
+    def part_dot(k):
+        def step(i, carry):
+            at = pl.ds(pl.multiple_of(i * 4 * TILE, TILE), 4 * TILE)
+            dz[k * 112 : (k + 1) * 112, at] = dot_nn(
+                turned(k)[0:112], cat[k * hid : (k + 1) * hid, at]
+            ).astype(LOW)
+            return carry
+
+        lax.fori_loop(0, tiles // 4, step, 0)
+        part_save(k).start()
 
     for t in range(2):
         soft_load(t).start()
@@ -824,11 +861,11 @@
                     functools.partial(back_dot, k, after, 1 - slot, 0),
                     functools.partial(back_dot, k, after, 1 - slot, 1),
                     functools.partial(sum_dot, k, before, 1 - slot),
-                    functools.partial(part_dot, k, before, 1 - slot),
                 ]
+                cuts = [0, 3 * hid // 8, 6 * hid // 8, hid]
                 for n, part in enumerate(parts):
                     part()
-                    for r in range(n * hid // 4, (n + 1) * hid // 4, CHUNK):
+                    for r in range(*cuts[n : n + 2], CHUNK):
                         rows = slice(r, r + CHUNK)
                         wide_rows = slice(k * hid + r, k * hid + r + CHUNK)
                         sums = [0.0, 0.0]
@@ -844,7 +881,9 @@
                             )
                             sums[0] += d * m2
                             sums[1] += da * m1
-                            wp[slot, rows, lanes] = v.astype(LOW)
+                            v = v.astype(LOW)
+                            wp[slot, rows, lanes] = v
+                            cat[wide_rows, pl.ds(pl.multiple_of(j * TILE + half * 128, 128), 128)] = v
                         acc[0, rows, :] += sums[0]
                         acc[1, rows, :] += sums[1]
 
@@ -856,8 +895,6 @@
 
         lax.fori_loop(0, groups, backward, 0)
         sum_dot(k, tiles - 1, 1)
-        part_dot(k, tiles - 1, 1)
-        part_save(k).start()
 
         two = lax.broadcasted_iota(jnp.int32, (hid, FP), 1)
         sl2 = jnp.sum(acc[0], axis=1, keepdims=True) * -LN2
@@ -869,13 +906,7 @@
         to_sibling(9 + k, pgrad.at[k % 2, :, 1 - core], pgrad_sib.at[k]).start()
 
         if k == 0:
-            to_sibling(8, wm_all.at[:, 0], wm_all.at[:, 1]).wait()
-            for c in range(nch):
-                v = mid_z[c * rb : (c + 1) * rb, 0:width_m] + wm_all[c, 1].astype(WIDE)
-                wm_all[c, 0] = v.astype(LOW)
-            for s in range(1, nch):
-                to_peer(8, s, wm_all.at[lax.rem(chip + s, nch), 0], gm_in.at[chip]).start()
-            gm_in[chip] = wm_all[chip, 0]
+            mid_add(K - 1)
             spread_two(7, head_all)
         if k == 1:
             spread_wait(7, head_all)
@@ -884,16 +915,17 @@
             reduce_two(9 + k - 1, pgrad.at[(k - 1) % 2], pgrad_sib.at[k - 1], pgrad_in.at[k - 1])
 
     k = K - 1
+    part_dot(0)
     to_sibling(9 + k, pgrad.at[k % 2, :, 1 - core], pgrad_sib.at[k]).wait()
     reduce_two(9 + k, pgrad.at[k % 2], pgrad_sib.at[k], pgrad_in.at[k])
-    for s in range(1, nch):
-        to_peer(8, s, wm_all.at[lax.rem(chip + s, nch), 0], gm_in.at[chip]).wait()
+    part_dot(1)
+    part_dot(2)
+    for c in range(K):
+        for s in range(1, nch):
+            mid_send(c, s).wait()
     gm_out[...] = total_of(gm_in)
     for k in range(K - 2, K):
         reduce_wait(9 + k, pgrad.at[k % 2], pgrad_in.at[k])
-
-    for k in range(K):
-        part_save(k).wait()
 
     lane_s = lax.broadcasted_iota(jnp.int32, (rb, FP), 1)
     quant = []
@@ -918,8 +950,11 @@
     rows_own[...] = quant[0:8, :]
     rows_all[chip, core] = rows_own[...]
     spread_one(13, rows_all)
+    part_dot(3)
     spread_two(13, rows_all)
     spread_wait(13, rows_all)
+    for k in range(K):
+        part_save(k).wait()
     full = []
     per = FP // rb
     lane8 = lax.broadcasted_iota(jnp.int32, (8, FP), 1)
@@ -971,8 +1006,8 @@
     *refs,
 ):
     states, outs = refs[:9], refs[9:]
-    grad_ref, logit_ref, grad_b, grad_h = outs[:4]
-    new = outs[4:]
+    grad_ref, logit_ref, grad_b, grad_h, grad_m = outs[:5]
+    new = outs[5:]
     width = feats_ref.shape[1]
     lane = lax.broadcasted_iota(jnp.int32, (1, width), 1) + pl.program_id(0) * width
     here = (lane < count_ref[0]).astype(WIDE)
@@ -992,6 +1027,7 @@
         g = jnp.concatenate([gb_ref[k][:, 0:F] for k in range(K)], axis=1)
         grad_b[...] = g
         grad_h[...] = gh_ref[0:C, :]
+        grad_m[...] = gm_ref[...]
         for n, (grad, rate) in enumerate(
             ((g, 0.8 / root), (gm_ref[...], 0.08 / root), (gh_ref[0:C, :], 0.3 / root))
         ):
@@ -1027,7 +1063,6 @@
     rows_g = K * FP // devices
     rows_h = 8
     feats = features.T
-    code = jnp.where(labelled > 0, labels, -1).reshape(1, nodes)
     small_rows = -(-small_params.shape[0] // (8 * FP)) * 8
     small = jnp.pad(small_params, (0, small_rows * FP - small_params.shape[0])).reshape(
         small_rows, FP
@@ -1048,7 +1083,7 @@
             jax.ShapeDtypeStruct((small_rows, FP), WIDE),
             jax.ShapeDtypeStruct((K, FP, FP), LOW),
         ),
-        in_specs=[smem, hbm] + [vmem] * 5,
+        in_specs=[smem, hbm] + [vmem] * 6,
         out_specs=(hbm, hbm, hbm, vmem, vmem, vmem, vmem, vmem),
         scratch_shapes=[
             pltpu.VMEM((K, FP, nodes), LOW),
@@ -1093,13 +1128,13 @@
             pltpu.SemaphoreType.DMA((2,)),
             pltpu.SemaphoreType.DMA((K,)),
             pltpu.SemaphoreType.DMA((2,)),
-            pltpu.SemaphoreType.DMA((14, nch)),
-            pltpu.SemaphoreType.DMA((14, nch)),
+            pltpu.SemaphoreType.DMA((17, nch)),
+            pltpu.SemaphoreType.DMA((17, nch)),
         ],
         compiler_params=pltpu.CompilerParams(
             collective_id=0, has_side_effects=True, vmem_limit_bytes=65400 * 1024
         ),
-    )(counts, feats, code, w_branch.T, w_mid.T, w_head.T, small)
+    )(counts, feats, labels.reshape(1, nodes), labelled.reshape(1, nodes), w_branch.T, w_mid.T, w_head.T, small)
     step = nodes // 2
     root = math.sqrt(nodes * devices)
 
@@ -1117,8 +1152,8 @@
         mom_head.T,
         avg_head.T,
     )
-    shapes = [jax.ShapeDtypeStruct(v.shape, WIDE) for v in (states[0], states[6]) + states]
-    fgrad, logits, grad_b, grad_h, *new = pl.pallas_call(
+    shapes = [jax.ShapeDtypeStruct(v.shape, WIDE) for v in (states[0], states[6], gm) + states]
+    fgrad, logits, grad_b, grad_h, grad_m, *new = pl.pallas_call(
         functools.partial(finish_kernel, root),
         grid=(nodes // step,),
         out_shape=[
@@ -1148,7 +1183,7 @@
         logits.T,
         fgrad.T,
         grad_b.T,
-        gm.T,
+        grad_m.T,
         grad_h.T,
         grad_small,
         mom_b,

time: 215 us -> 208 us (0.967)
  Pallas kernels: 207 us -> 203 us
    pallas_call x1, Pallas kernels: 199 us -> 195 us  [fused(): pl.pallas_call(functools.partial(net_kernel, nch), out_shape=(jax.ShapeDt...]
where the time goes in v3:
time: 208 us
  Pallas kernels  203 us (98%)
    pallas_call x1, Pallas kernels, fused(): pl.pallas_call(functools.partial(net_kernel, nch), out_shape=(jax.ShapeDt...  195 us
    pallas_call x1, Pallas kernels, fused(): pl.pallas_call(functools.partial(finish_kernel, root), grid=(nodes // ste...  8.5 us

profile of v3, /device:TPU:0, one launch (start us, length us, event | category | flops | bytes accessed | tf_op | source)
XLA Modules:
  0.0 207.8 jit_solution(14387141318353019551)
XLA Ops:
  1.3 1.4 pad_bitcast_fusion.small_ref
  2.7 194.9 %shard_map.295 = (f32[48,5120]{1,0:T(8,128)}, bf16[4,112,5120]{2,1,0:T(8,128)(2,1)}, bf16[2,20,4,512,256]{4,3,2,1,0:T(8,128)(2,1)}, f32[16,2048]{1,0:T(8,128)}, ...) custom-call(s32[1]{0:T(128)S(6)} %copy.34.count_ref, ...), custom_call_target="tpu_custom_call" | custom-call | tf_op jit(solution)/shard_map/pallas_call | solution.py:1074
  197.6 1.5 multiply_add_fusion
  199.1 8.5 %shard_map.296 = (f32[400,5120]{1,0:T(8,128)}, f32[47,5120]{1,0:T(8,128)}, f32[16,400]{1,0:T(8,128)}, f32[47,512]{1,0:T(8,128)}, f32[16,2048]{1,0:T(8,128)}, /*i...) custom-call(s32[1]{0:T(128)S(6)} %copy.34.count_ref, ...), custom_call_target="tpu_custom_call" | custom-call | tf_op jit(solution)/shard_map/pallas_call | solution.py:1156
